TPU v7x, 32 devices: a whole 2x2x4 slice. The times are simulated.
32 devices in a mesh: group: 2 (over y), patch: 4 (over z), tensor: 2 (over x), seq: 2 (over core).
Axes of the slice: x: 2, y: 2, z: 4, core: 2. Of those that a mesh axis runs over, the one named last changes fastest.
Arguments:
- query_raw: bfloat16 [6144, 1536], P(('group', 'patch', 'seq'), 'tensor'), parts along dimension 0, may hold values from -6 to 6
- key_raw: bfloat16 [6144, 1536], P(('group', 'patch', 'seq'), 'tensor'), parts along dimension 0, may hold values from -6 to 6
- value_raw: bfloat16 [6144, 1536], P(('group', 'patch', 'seq'), 'tensor'), parts along dimension 0, may hold values from -6 to 6
- key_cache: bfloat16 [6144, 1536], P(('group', 'patch', 'seq'), 'tensor'), parts along dimension 0, may hold values from -4 to 4
- value_cache: bfloat16 [6144, 1536], P(('group', 'patch', 'seq'), 'tensor'), parts along dimension 0, may hold values from -4 to 4
- norm_gain: float32 [2, 2, 128], replicated, may hold values from 0.5 to 3
- layout: int32 [2, 6144], P(None, ('group', 'patch', 'seq')), parts along dimension 1, may hold values from 0 to 352, as said below
- group_size: int32 [12], P('tensor'), may hold values from 64 to 128, as said below
- step_index: int32 [2], P('group'), parts along dimension 0, may hold values from 0 to 27
- gate_table: float32 [2, 28, 3072], P(None, None, 'seq'), may hold values from -4 to 4
- out_weight: bfloat16 [2, 1536, 3072], P(None, 'tensor', 'seq'), may hold values from -0.15625 to 0.15625
Outputs:
- block_out: bfloat16 [6144, 3072], P(('group', 'patch', 'tensor'), 'seq'), parts along dimension 0
- key_next: bfloat16 [6144, 1536], P(('group', 'patch', 'seq'), 'tensor'), parts along dimension 0
- value_next: bfloat16 [6144, 1536], P(('group', 'patch', 'seq'), 'tensor'), parts along dimension 0
There are 2 independent parts, one for each index of `group`. A program takes and returns all parts, laid end to end along the dimension named above; an argument that names none is the same for every part. Nothing has to cross between parts.
Inputs may be any that keep to these rules, and one draw needn't show every extreme that they name: `layout`: the first 256 tokens (text) have both ids 0; image token j takes row j // w + s and column c + (j % w) or c + w - 1 - (j % w) (one direction for the whole image) of a raster whose width w, 8 to 63, column offset c of at least 1, and direction are drawn for each image, with the row offset s of at least 1 chosen so that the last image token's row is the largest id; no column id exceeds it. `group_size`: each entry is 128 or 64; half of the heads take each.
All inputs are finite; a program needn't handle non-finite values.
Results may differ from a plain program's by a relative error of at most 0.03.
Values may be sent and summed in bfloat16 or wider, within the bound.
A program may use at most 128 MiB of HBM per device.

v0:
```python
import jax
import jax.numpy as jnp
from jax import lax
from jax.sharding import PartitionSpec as P

RA = 16
RB = 56


rope_theta = 10000.0
norm_eps = 1e-06


def rope_tables(positions, plain_dims, rotary_dims):
    half_len = rotary_dims // 2
    exponent = jnp.arange(half_len, dtype=jnp.float32) * (2.0 / rotary_dims)
    freqs = jnp.exp(-jnp.log(rope_theta) * exponent)
    token_count = positions.shape[1]
    cosine = [jnp.ones((token_count, plain_dims), jnp.float32)]
    sine_part = [jnp.zeros((token_count, plain_dims), jnp.float32)]
    for which in range(2):
        angle = positions[which].astype(jnp.float32)[:, None] * freqs[None, :]
        cosine += [jnp.cos(angle), jnp.cos(angle)]
        sine_part += [jnp.sin(angle), jnp.sin(angle)]
    return (jnp.concatenate(cosine, 1), jnp.concatenate(sine_part, 1))


def partner(values, plain_dims, rotary_dims):
    half_len = rotary_dims // 2
    second = plain_dims + rotary_dims
    return jnp.concatenate(
        [
            values[..., :plain_dims],
            -values[..., plain_dims + half_len : second],
            values[..., plain_dims : plain_dims + half_len],
            -values[..., second + half_len :],
            values[..., second : second + half_len],
        ],
        -1,
    )


def compress(residual, group_size, heads, head_dim):
    row_count = residual.shape[0]
    halves = residual.reshape(row_count, heads, 2, head_dim // 2)
    half_ms = jnp.mean(halves * halves, -1)
    whole_ms = jnp.mean(half_ms, -1, keepdims=True)
    whole = (group_size == head_dim)[None, :, None]
    mean_sq = jnp.where(whole, whole_ms, half_ms)
    scales = jnp.sqrt(mean_sq + norm_eps).astype(jnp.bfloat16)
    codes = jnp.tanh(halves / scales.astype(jnp.float32)[..., None]).astype(jnp.bfloat16)
    return (codes.reshape(row_count, heads * head_dim), scales.reshape(row_count, heads * 2))


def decode(codes, scales, heads, head_dim):
    row_count = codes.shape[0]
    parts = codes.astype(jnp.float32).reshape(row_count, heads, 2, head_dim // 2) * scales.astype(
        jnp.float32
    ).reshape(row_count, heads, 2, 1)
    return parts.reshape(row_count, heads * head_dim)


def prepare(query_raw, key_raw, value_raw, positions, norm_gain, key_rows, value_rows, group_size):
    row_count = query_raw.shape[0]
    heads = group_size.shape[0]
    head_dim = norm_gain.shape[-1]
    text_rows = (positions[0] == 0)[:, None, None]
    cosine, sine_part = rope_tables(positions, RA, RB)
    cosine = cosine[:, None, :]
    sine_part = sine_part[:, None, :]

    def embed(raw, which):
        gain = jnp.where(
            text_rows, norm_gain[0, which][None, None, :], norm_gain[1, which][None, None, :]
        )
        values = raw.astype(jnp.float32).reshape(row_count, heads, head_dim)
        normed = values * lax.rsqrt(jnp.mean(values * values, -1, keepdims=True) + norm_eps) * gain
        return (normed * cosine + partner(normed, RA, RB) * sine_part).reshape(
            row_count, heads * head_dim
        )

    query_rot = embed(query_raw, 0).astype(jnp.bfloat16)
    key_rot = embed(key_raw, 1)
    key_codes, key_scales = compress(
        key_rot - key_rows.astype(jnp.float32), group_size, heads, head_dim
    )
    value_codes, value_scales = compress(
        value_raw.astype(jnp.float32) - value_rows.astype(jnp.float32), group_size, heads, head_dim
    )
    return (query_rot, key_codes, value_codes, key_scales, value_scales)


def block_length(piece_rows):
    for candidate in range(min(piece_rows, 2048), 0, -1):
        if piece_rows % candidate == 0:
            return candidate
    return piece_rows


def on_device(
    query_raw,
    key_raw,
    value_raw,
    key_cache,
    value_cache,
    norm_gain,
    layout,
    group_size,
    step_index,
    gate_table,
    out_weight,
):
    row_count = query_raw.shape[0]
    heads = group_size.shape[0]
    head_dim = norm_gain.shape[-1]
    query_rot, key_codes, value_codes, key_scales, value_scales = prepare(
        query_raw, key_raw, value_raw, layout, norm_gain, key_cache, value_cache, group_size
    )
    key_mine = (
        key_cache.astype(jnp.float32) + decode(key_codes, key_scales, heads, head_dim)
    ).astype(jnp.bfloat16)
    value_mine = (
        value_cache.astype(jnp.float32) + decode(value_codes, value_scales, heads, head_dim)
    ).astype(jnp.bfloat16)
    query_heads = query_rot.reshape(row_count, heads, head_dim)
    inverse_root = head_dim ** (-0.5)
    start_state = (
        jnp.zeros((heads, row_count, head_dim), jnp.float32),
        jnp.zeros((heads, row_count), jnp.float32),
    )
    keys_all = lax.all_gather(key_mine, ("patch", "seq"), axis=0, tiled=True)
    values_all = lax.all_gather(value_mine, ("patch", "seq"), axis=0, tiled=True)
    piece_rows = keys_all.shape[0]
    length = block_length(piece_rows)

    def one_block(index, carry):
        numer, totals = carry
        keys = lax.dynamic_slice_in_dim(keys_all, index * length, length, 0).reshape(
            length, heads, head_dim
        )
        values = lax.dynamic_slice_in_dim(values_all, index * length, length, 0).reshape(
            length, heads, head_dim
        )
        scores = (
            jnp.einsum("qhd,khd->hqk", query_heads, keys, preferred_element_type=jnp.float32)
            * inverse_root
        )
        weights = jnp.exp(scores)
        totals = totals + jnp.sum(weights, -1)
        numer = numer + jnp.einsum(
            "hqk,khd->hqd", weights.astype(jnp.bfloat16), values, preferred_element_type=jnp.float32
        )
        return (numer, totals)

    numer, totals = lax.fori_loop(0, piece_rows // length, one_block, start_state)
    attn_rows = (
        (numer / totals[..., None])
        .transpose(1, 0, 2)
        .reshape(row_count, heads * head_dim)
        .astype(jnp.bfloat16)
    )
    text_flag = (layout[0] == 0).astype(jnp.bfloat16)
    pair_attn, pair_text = (
        lax.all_gather(attn_rows, "seq", axis=0, tiled=True),
        lax.all_gather(text_flag, "seq", axis=0, tiled=True),
    )
    share = pair_attn.shape[0] // lax.axis_size("tensor")

    def both_streams(block, block_text):
        text_part = jnp.dot(block, out_weight[0], preferred_element_type=jnp.float32)
        image_part = jnp.dot(block, out_weight[1], preferred_element_type=jnp.float32)
        return jnp.where(block_text[:, None] > 0, text_part, image_part)

    def image_only(block, block_text):
        return jnp.dot(block, out_weight[1], preferred_element_type=jnp.float32)

    block = pair_attn
    block_text = pair_text
    projected = lax.psum_scatter(
        lax.cond(jnp.any(block_text > 0), both_streams, image_only, block, block_text),
        "tensor",
        scatter_dimension=0,
        tiled=True,
    )
    mine_text = lax.dynamic_slice_in_dim(pair_text, lax.axis_index("tensor") * share, share, 0)
    chosen = (jnp.arange(gate_table.shape[1]) == step_index[0]).astype(jnp.float32)
    gates = jnp.sum(gate_table * chosen[None, :, None], 1)
    gate_rows = jnp.where(mine_text[:, None] > 0, gates[0][None, :], gates[1][None, :])
    return ((gate_rows * projected).astype(jnp.bfloat16), key_mine, value_mine)


def solution(mesh):
    in_specs = (
        P(("group", "patch", "seq"), "tensor"),
        P(("group", "patch", "seq"), "tensor"),
        P(("group", "patch", "seq"), "tensor"),
        P(("group", "patch", "seq"), "tensor"),
        P(("group", "patch", "seq"), "tensor"),
        P(),
        P(None, ("group", "patch", "seq")),
        P("tensor"),
        P("group"),
        P(None, None, "seq"),
        P(None, "tensor", "seq"),
    )
    out_specs = (
        P(("group", "patch", "tensor"), "seq"),
        P(("group", "patch", "seq"), "tensor"),
        P(("group", "patch", "seq"), "tensor"),
    )
    return jax.shard_map(
        on_device, mesh=mesh, in_specs=in_specs, out_specs=out_specs, check_vma=False
    )
```

profile of v0, /device:TPU:0, one launch (start us, length us, event | category | flops | bytes accessed | tf_op | source)
XLA Modules:
  0.0 294.3 jit_solution(1301954242473785097)
XLA Ops:
  7.2 0.8 slice_bitcast_fusion.1
  8.0 0.7 compare_reduce_fusion
  8.7 1.4 copy.34
  10.1 0.1 multiply_reduce_fusion.1
  10.2 0.9 copy-done.7
  11.1 0.3 copy.35
  11.4 0.1 multiply_reduce_fusion
  11.6 0.1 broadcast_select_fusion
  11.8 0.3 multiply_multiply_fusion
  12.0 0.2 copy-done.10
  12.2 0.2 copy-done.5
  12.4 0.1 fusion.26
  12.5 0.7 slice.85
  13.2 1.0 fusion.25
  14.2 0.7 slice.90
  14.8 0.6 convert_reduce_fusion
  15.4 0.5 multiply_exponential_fusion.1
  16.0 1.4 copy.33
  17.3 1.7 multiply_cosine_fusion
  19.0 0.6 broadcast_in_dim.149
  19.6 7.1 %concatenate.14 = f32[384,128]{0,1:T(8,128)} concatenate(f32[384,16]{0,1:T(8,128)} %broadcast_in_dim.149, f32[384,28]{0,1:T(8,128)} %get-tuple-element.236, f32[384,28]{0,1:T(8,128)} %get-tuple-element.236, f32[384,28]{0,1:T(8,128)} %get-tuple-element.225, f32[384,28]{0,1:T(8,128)} %get-tuple-element.225), dimensions={1} | concatenate | bytes 393216 | tf_op jit(solution)/shard_map/concatenate | solution.py:25
  26.7 7.6 %concatenate.13 = f32[384,6,128]{0,2,1:T(8,128)} concatenate(f32[384,6,16]{0,2,1:T(8,128)} %slice.85, f32[384,6,28]{0,2,1:T(8,128)S(1)} %get-tuple-element.219, f32[384,6,28]{0,2,1:T(8,128)S(1)} %get-tuple-element.218, f32[384,6,28]{0,2,1:T(8,128)S(1)} %get-tuple-element.217, f32[384,6,28]{0,2,1:T(8,128)S(1)} %get-tuple-element.216), dimensions={2} | concatenate | bytes 2359296 | tf_op jit(solution)/shard_map/concatenate | solution.py:31
  34.3 9.5 %concatenate.15 = f32[384,6,128]{0,2,1:T(8,128)} concatenate(f32[384,6,16]{0,2,1:T(8,128)} %slice.90, f32[384,6,28]{0,2,1:T(8,128)} %get-tuple-element.215, f32[384,6,28]{0,2,1:T(8,128)} %get-tuple-element.214, f32[384,6,28]{0,2,1:T(8,128)} %get-tuple-element.213, f32[384,6,28]{0,2,1:T(8,128)S(1)} %get-tuple-element.212), dimensions={2} | concatenate | bytes 2359296 | tf_op jit(solution)/shard_map/concatenate | solution.py:31
  43.8 2.9 broadcast_multiply_fusion
  46.8 0.3 concatenate.12
  47.1 1.3 fusion.22
  48.4 1.4 reduce_sum.78
  49.9 0.6 copy-done.9
  50.4 0.6 broadcast_multiply_fusion.3
  51.0 1.4 copy.36
  52.4 2.1 copy.37
  54.5 2.2 fusion.21
  56.8 2.0 reduce_sum.81
  58.7 0.8 multiply_reduce_fusion.3
  59.5 1.5 fusion.24
  61.0 2.2 fusion.13
  63.3 3.1 %fusion.16 = (bf16[384,768]{0,1:T(8,128)(2,1)S(1)}, bf16[384,768]{0,1:T(8,128)(2,1)}) fusion(f32[384,6,128]{0,2,1:T(8,128)} %get-tuple-element.222, f32[384,128]{0,1:T(8,128)} %copy-done.5, f32[384,6]{0,1:T(8,128)} %copy-done.10, f32[384,128]{0,1:T(8,128)} %copy-done.6, bf16[384,768]{0,1:T(8,128)(2,1)S(1)} %copy.35, f32[384,6,2]{0,2,1:T(2,128)} %get-tuple-element.233, ...), kind=kLoop, calls=%fused_computation.35 | loop fusion | flops 5603328 | bytes 5935104 | tf_op jit(solution)/shard_map/convert_element_type | solution.py:82
  66.4 0.2 all-gather.9.cloned.1.call-start
  66.7 1.1 copy.38
  67.7 49.9 %all-gather.7.cloned.1.call-done = bf16[3072,768]{0,1:T(8,128)(2,1)} async-done(((bf16[384,768]{0,1:T(8,128)(2,1)}), bf16[3072,768]{0,1:T(8,128)(2,1)}) %all-gather.7.cloned.1.call-update) | async-done | bytes 4718608 | tf_op jit(solution)/shard_map/all_gather | solution.py:132
  117.6 52.4 %all-gather.5.cloned.1.call-done = bf16[3072,768]{0,1:T(8,128)(2,1)} async-done(((bf16[384,768]{0,1:T(8,128)(2,1)}), bf16[3072,768]{0,1:T(8,128)(2,1)}) %all-gather.5.cloned.1.call-update) | async-done | bytes 4718608 | tf_op jit(solution)/shard_map/all_gather | solution.py:131
  170.0 37.1 %while.16 = (s32[]{:T(128)}, f32[6,384,128]{2,1,0:T(8,128)S(1)}, f32[6,384]{1,0:T(8,128)}, bf16[3072,768]{0,1:T(8,128)(2,1)}, bf16[384,6,128]{2,0,1:T(8,128)(2,1...) while((s32[]{:T(128)}, f32[6,384,128]{2,1,0:T(8,128)S(1)}, ...), condition=%wide.region_10.11_spmd.clone, body=%wide.region_8.10_spmd.clone.sunk | while | flops 1826687232 | bytes 47812796 | solution.py:155
  170.0 2.7 constant_dynamic-slice_fusion.3
  172.8 6.6 %bitcast_reduce_fusion.2 = (f32[6,384]{1,0:T(8,128)S(1)}, f32[6,1536,384]{2,1,0:T(8,128)}) fusion(bf16[1536,6,128]{0,2,1:T(8,128)(2,1)S(1)} %bitcast.126, bf16[384,6,128]{2,0,1:T(8,128)(2,1)S(1)} %copy-done), kind=kOutput, calls=%fused_computation.10.clone.1 | convolution fusion | flops 913045248 | bytes 17114112 | tf_op jit(solution)/shard_map/while/body/eval_jaxpr/qhd,khd->hqk/dot_general | solution.py:145
  179.4 8.2 %fusion.40 = f32[6,384,128]{2,1,0:T(8,128)S(1)} fusion(bf16[1536,6,128]{0,2,1:T(8,128)(2,1)S(1)} %bitcast.127, f32[6,1536,384]{2,1,0:T(8,128)} %get-tuple-element.283, f32[6,384,128]{2,1,0:T(8,128)S(1)} %get-tuple-element.296, pred[]{:T(512)S(6)} %compare.3), kind=kOutput, calls=%fused_computation.15.clone.1 | convolution fusion | flops 913637376 | bytes 18874368 | tf_op jit(solution)/shard_map/while/body/eval_jaxpr/hqk,khd->hqd/dot_general | solution.py:150
  187.6 0.6 select_add_fusion.2
  188.2 2.7 constant_dynamic-slice_fusion.3
  191.0 6.6 %bitcast_reduce_fusion.2 = (f32[6,384]{1,0:T(8,128)S(1)}, f32[6,1536,384]{2,1,0:T(8,128)}) fusion(bf16[1536,6,128]{0,2,1:T(8,128)(2,1)S(1)} %bitcast.126, bf16[384,6,128]{2,0,1:T(8,128)(2,1)S(1)} %copy-done), kind=kOutput, calls=%fused_computation.10.clone.1 | convolution fusion | flops 913045248 | bytes 17114112 | tf_op jit(solution)/shard_map/while/body/eval_jaxpr/qhd,khd->hqk/dot_general | solution.py:145
  197.6 8.2 %fusion.40 = f32[6,384,128]{2,1,0:T(8,128)S(1)} fusion(bf16[1536,6,128]{0,2,1:T(8,128)(2,1)S(1)} %bitcast.127, f32[6,1536,384]{2,1,0:T(8,128)} %get-tuple-element.283, f32[6,384,128]{2,1,0:T(8,128)S(1)} %get-tuple-element.296, pred[]{:T(512)S(6)} %compare.3), kind=kOutput, calls=%fused_computation.15.clone.1 | convolution fusion | flops 913637376 | bytes 18874368 | tf_op jit(solution)/shard_map/while/body/eval_jaxpr/hqk,khd->hqd/dot_general | solution.py:150
  205.8 1.3 select_add_fusion.2
  207.1 0.4 copy.39
  207.5 1.6 divide_convert_fusion
  209.2 1.8 all-gather
  211.0 0.6 compare_reduce_fusion.1
  212.3 4.9 %all-gather.9.cloned.1.call-done = bf16[768,768]{0,1:T(8,128)(2,1)} async-done(((bf16[384,768]{0,1:T(8,128)(2,1)}), bf16[768,768]{0,1:T(8,128)(2,1)}) %all-gather.9.cloned.1.call-update) | async-done | bytes 1179664 | tf_op jit(solution)/shard_map/all_gather | solution.py:164
  217.2 8.4 %conditional.1 = (f32[768,1536]{1,0:T(8,128)}) conditional(s32[]{:T(128)} %convert_element_type.130, (bf16[2,768,1536]{2,1,0:T(8,128)(2,1)}, bf16[768,768]{0,1:T(8,128)(2,1)}) %tuple.29, (bf16[768]{0:T(1024)(128)(2,1)S(1)}, bf16[2,768,1536]{2,1,0:T(8,128)(2,1)}, bf16[768,768]{0,1:T(8,128)(2,1)}) %tuple.30), branch_computations={%region_11.12_spmd, %region_12.13_spmd} | conditional | flops 3625059072 | bytes 40111444 | solution.py:180
  217.2 4.2 %fusion.4 = f32[768,1536]{1,0:T(8,128)S(1)} fusion(bf16[768,768]{0,1:T(8,128)(2,1)} %get-tuple-element.184, bf16[2,768,1536]{2,1,0:T(8,128)(2,1)} %get-tuple-element.125), kind=kOutput, calls=%fused_computation.5 | convolution fusion | flops 1811939328 | bytes 8257536 | tf_op jit(solution)/shard_map/cond/branch_1_fun/dot_general | solution.py:170
  221.5 4.2 %convolution_select_fusion = f32[768,1536]{1,0:T(8,128)} fusion(f32[768,1536]{1,0:T(8,128)S(1)} %fusion.4, bf16[768,768]{0,1:T(8,128)(2,1)S(1)} %copy-done.4, bf16[2,768,1536]{2,1,0:T(8,128)(2,1)S(1)} %bitcast.135, pred[768]{0:T(1024)(128)(4,1)S(1)} %broadcast_compare_fusion), kind=kOutput, calls=%fused_computation.3 | convolution fusion | flops 1813118976 | bytes 12977152 | tf_op jit(solution)/shard_map/cond/branch_1_fun/dot_general | solution.py:171
  225.7 1.0 copy-done.1
  226.7 1.1 copy.43
  227.8 1.1 copy.42
  229.6 0.2 multiply_reduce_fusion.2
  229.9 54.9 %reduce-scatter.2.cloned.1.call-done = f32[384,1536]{1,0:T(8,128)} async-done(((f32[768,1536]{1,0:T(8,128)}), f32[384,1536]{1,0:T(8,128)}) %reduce-scatter.2.cloned.1.call-update) | async-done | bytes 2359312 | tf_op jit(solution)/shard_map/reduce_scatter | solution.py:179
  284.8 3.0 %multiply_convert_fusion = bf16[384,1536]{1,0:T(8,128)(2,1)} fusion(f32[384,1536]{1,0:T(8,128)} %reduce-scatter.2.cloned.1.call-done, f32[1536]{0:T(1024)S(1)} %get-tuple-element.189, f32[1536]{0:T(1024)S(1)} %get-tuple-element.188, pred[384]{0:T(512)(128)(4,1)S(1)} %dynamic-slice_compare_fusion), kind=kLoop, calls=%fused_computation.20 | loop fusion | flops 1769472 | bytes 3551616 | tf_op jit(solution)/shard_map/convert_element_type | solution.py:189
  (55 shorter events, 0.5 us)
Async XLA Ops:
  7.2 110.4 %all-gather.7.cloned.1.call-start = ((), (), s32[]{:S(2)}) async-start(), calls=%async_computation.2 | async-start | bytes 5308416 | tf_op jit(solution)/shard_map/all_gather | solution.py:132
  8.7 2.9 copy-start.12
  10.1 1.1 copy-start.7
  11.6 0.6 copy-start.10
  11.7 0.7 copy-start.5
  11.8 35.3 %copy-start.3 = (f32[384,128]{0,1:T(8,128)}, f32[384,128]{0,1:T(8,128)S(1)}, u32[]{:S(2)}) copy-start(f32[384,128]{0,1:T(8,128)S(1)} %get-tuple-element.235) | copy-start | bytes 589828
  13.2 1.6 copy-start.11
  47.1 1.4 copy-start.6
  49.8 0.6 copy-start.9
  56.8 2.7 copy-start.14
  63.2 106.8 %all-gather.5.cloned.1.call-start = ((), (), s32[]{:S(2)}) async-start(), calls=%async_computation.1 | async-start | bytes 5308416 | tf_op jit(solution)/shard_map/all_gather | solution.py:131
  66.4 150.8 %all-gather.9.cloned.1.call-start = ((), (), s32[]{:S(2)}) async-start(), calls=%async_computation.3 | async-start | bytes 1769472 | tf_op jit(solution)/shard_map/all_gather | solution.py:164
  170.0 2.7 copy-start
  188.2 2.7 copy-start
  207.5 1.7 copy-start.13
  209.1 75.7 %reduce-scatter.2.cloned.1.call-start = ((), (), s32[]{:S(2)}) async-start(), calls=%async_computation.4 | async-start | bytes 7077888 | tf_op jit(solution)/shard_map/reduce_scatter | solution.py:179
  217.2 4.2 %slice-start = ((s8[4718592]{0:T(1024)(128)(4,1)}), s8[4194304]{0:T(1024)(128)(4,1)S(1)}, s32[]{:S(2)}) async-start(s8[4718592]{0:T(1024)(128)(4,1)} %bitcast.134), calls=%async_computation.5 | async-start | bytes 8388608 | tf_op jit(solution)/shard_map/cond
  217.2 4.2 %copy-start.4 = (bf16[768,768]{0,1:T(8,128)(2,1)S(1)}, bf16[768,768]{0,1:T(8,128)(2,1)}, u32[]{:S(2)}) copy-start(bf16[768,768]{0,1:T(8,128)(2,1)} %get-tuple-element.184) | copy-start | bytes 3538948 | tf_op jit(solution)/shard_map/cond
  217.2 4.2 %slice-start.1 = ((s8[4718592]{0:T(1024)(128)(4,1)}), s8[524288]{0:T(1024)(128)(4,1)S(1)}, s32[]{:S(2)}) async-start(s8[4718592]{0:T(1024)(128)(4,1)} %bitcast.134), calls=%async_computation.6 | async-start | bytes 1048576 | tf_op jit(solution)/shard_map/cond
  225.6 1.1 copy-start.1
  225.7 2.1 copy-start.2
  226.7 2.9 copy-start.8
Sparse Core Ops, SparseCore 0:
  63.3 54.1 all-gather.6
  119.8 50.2 all-gather.4
  209.2 7.9 all-gather.8
  225.8 58.9 reduce-scatter.1
where the time goes:
time: 296 us; the launch traced here: 294 us
  waiting for transfers between devices  162 us (55%)
  local copies, waits for them, and re-layouts  45.8 us (15%)
  matrix products  38 us (13%)
  other arithmetic  30.7 us (10%)
  between operations  15.4 us (5%)
    reduce_scatter x1, waiting for transfers between devices, on_device(): lax.psum_scatter(lax.cond(jnp.any(block_text > 0), both_streams, image_on...  54.9 us
    all_gather x1, waiting for transfers between devices, on_device(): keys_all = lax.all_gather(key_mine, ('patch', 'seq'), axis=0, tiled=True)  52.4 us
    all_gather x1, waiting for transfers between devices, on_device(): lax.all_gather(value_mine, ('patch', 'seq'), axis=0, tiled=True)  49.9 us
    concatenate x2, local copies, waits for them, and re-layouts, partner(): jnp.concatenate([values[..., :plain_dims], -values[..., plain_dims + half...  17.1 us
    dot_general x2, matrix products, one_block(): jnp.einsum('hqk,khd->hqd', weights.astype(jnp.bfloat16), values, preferre...  16.4 us
    dot_general x2, matrix products, one_block(): jnp.einsum('qhd,khd->hqk', query_heads, keys, preferred_element_type=jnp....  13.2 us
    unnamed x36, local copies, waits for them, and re-layouts  12.7 us
    concatenate x2, local copies, waits for them, and re-layouts, rope_tables(): return (jnp.concatenate(cosine, 1), jnp.concatenate(sine_part, 1))  7.37 us
  transfers between devices with their start and end apart: 4, of which 4 were waited for; matrix products, arithmetic and copies ran while one was open for 2% of the time, Pallas kernels for 0%

commit v1 on v0

--- a/solution.py
+++ b/solution.py
@@ -1,6 +1,11 @@
+import functools
+import math
 import jax
 import jax.numpy as jnp
+import numpy as np
 from jax import lax
+from jax.experimental import pallas as pl
+from jax.experimental.pallas import tpu as pltpu
 from jax.sharding import PartitionSpec as P
 
 RA = 16
@@ -189,6 +194,415 @@
     return ((gate_rows * projected).astype(jnp.bfloat16), key_mine, value_mine)
 
 
+MESH = pl.DeviceIdType.MESH
+GATHER_SHARE = 2
+
+
+def lane_tables(head_dim):
+    half_len = RB // 2
+    freqs = np.exp(-math.log(rope_theta) * np.arange(half_len) * (2.0 / RB)).astype(np.float32)
+    table = np.zeros((8, head_dim), np.float32)
+    for which in range(2):
+        start = RA + which * RB
+        table[which, start : start + half_len] = freqs
+        table[which, start + half_len : start + RB] = freqs
+        table[2, start : start + half_len] = -1.0
+        table[3, start + half_len : start + RB] = 1.0
+    return jnp.asarray(table)
+
+
+def split_dot(values, matrix):
+    high = values.astype(jnp.bfloat16)
+    low = (values - high.astype(jnp.float32)).astype(jnp.bfloat16)
+    return jnp.dot(
+        jnp.concatenate([high, low], 1),
+        jnp.concatenate([matrix, matrix], 0),
+        preferred_element_type=jnp.float32,
+    )
+
+
+def prepare_kernel(
+    sizes, positions, gains, table, query, key, value, key_old, value_old,
+    query_out, pair_out, key_out, value_out, cosine, sine_low, sine_high, gain_q, gain_k,
+):
+    head = pl.program_id(0)
+    head_dim = query.shape[1]
+    half_len = RB // 2
+
+    @pl.when(head == 0)
+    def _():
+        rows_id = positions[:, 0:1]
+        angle = rows_id * table[0:1, :] + positions[:, 1:2] * table[1:2, :]
+        sine = jnp.sin(angle)
+        cosine[...] = jnp.cos(angle)
+        sine_low[...] = sine * table[2:3, :]
+        sine_high[...] = sine * table[3:4, :]
+        text = rows_id == 0
+        gain_q[...] = jnp.where(text, gains[0:1, :], gains[2:3, :])
+        gain_k[...] = jnp.where(text, gains[1:2, :], gains[3:4, :])
+
+    full = jnp.full((head_dim, head_dim), 1.0 / head_dim, jnp.float32)
+    row = lax.broadcasted_iota(jnp.int32, (head_dim, head_dim), 0) < head_dim // 2
+    col = lax.broadcasted_iota(jnp.int32, (head_dim, head_dim), 1) < head_dim // 2
+    halves = jnp.where(row == col, 2.0 / head_dim, 0.0)
+    whole = (sizes[head] == head_dim).astype(jnp.float32)
+    grouped = (whole * full + (1.0 - whole) * halves).astype(jnp.bfloat16)
+    full = full.astype(jnp.bfloat16)
+
+    def embed(raw, gain):
+        values = raw[...].astype(jnp.float32)
+        normed = values * lax.rsqrt(split_dot(values * values, full) + norm_eps) * gain[...]
+        return (
+            normed * cosine[...]
+            + pltpu.roll(normed, head_dim - half_len, 1) * sine_low[...]
+            + pltpu.roll(normed, half_len, 1) * sine_high[...]
+        )
+
+    def update(fresh, old):
+        kept = old[...].astype(jnp.float32)
+        residual = fresh - kept
+        scale = jnp.sqrt(split_dot(residual * residual, grouped) + norm_eps)
+        scale = scale.astype(jnp.bfloat16).astype(jnp.float32)
+        code = jnp.tanh(residual / scale).astype(jnp.bfloat16).astype(jnp.float32)
+        return (kept + scale * code).astype(jnp.bfloat16)
+
+    query_out[0] = embed(query, gain_q).astype(jnp.bfloat16)
+    key_next = update(embed(key, gain_k), key_old)
+    value_next = update(value[...].astype(jnp.float32), value_old)
+    pair_out[0, 0] = key_next
+    pair_out[0, 1] = value_next
+    key_out[...] = key_next
+    value_out[...] = value_next
+
+
+def prepare_call(query, key, value, key_old, value_old, norm_gain, layout, group_size):
+    rows, width = query.shape
+    heads = group_size.shape[0]
+    hd = width // heads
+    block = pl.BlockSpec((rows, hd), lambda h: (0, h))
+    whole = lambda *shape: pl.BlockSpec(shape, lambda h: (0,) * len(shape))
+    return pl.pallas_call(
+        prepare_kernel,
+        grid=(heads,),
+        in_specs=[
+            pl.BlockSpec(memory_space=pltpu.SMEM),
+            whole(rows, 2),
+            whole(4, hd),
+            whole(8, hd),
+        ]
+        + [block] * 5,
+        out_specs=[
+            pl.BlockSpec((1, rows, hd), lambda h: (h, 0, 0)),
+            pl.BlockSpec((1, 2, rows, hd), lambda h: (h, 0, 0, 0)),
+            block,
+            block,
+        ],
+        out_shape=[
+            jax.ShapeDtypeStruct((heads, rows, hd), jnp.bfloat16),
+            jax.ShapeDtypeStruct((heads, 2, rows, hd), jnp.bfloat16),
+            jax.ShapeDtypeStruct((rows, width), jnp.bfloat16),
+            jax.ShapeDtypeStruct((rows, width), jnp.bfloat16),
+        ],
+        scratch_shapes=[pltpu.VMEM((rows, hd), jnp.float32)] * 5,
+        compiler_params=pltpu.CompilerParams(vmem_limit_bytes=32 * 2**20),
+    )(
+        group_size,
+        layout.astype(jnp.float32).T,
+        norm_gain.reshape(4, hd),
+        lane_tables(hd),
+        query,
+        key,
+        value,
+        key_old,
+        value_old,
+    )
+
+
+def attend_kernel(
+    query, pair, out, held, guest, mixed, returned, in_send, out_send, side_send, line_recv,
+    side_recv, guest_send, guest_recv, back_send, back_recv,
+):
+    heads, rows, hd = query.shape
+    shared = heads // GATHER_SHARE
+    chip = lax.axis_index("patch")
+    core = lax.axis_index("seq")
+    other_core = 1 - core
+    upper = chip // 2
+    is_end = (chip == 0) | (chip == 3)
+    is_mid = jnp.logical_not(is_end)
+    my_end = upper * 3
+    my_mid = 1 + upper
+    far_mid = 2 - upper
+    far_end = 3 - my_end
+    inner = jnp.where(is_end, my_mid, far_mid)
+    outer = my_end
+
+    def slot(source):
+        return source * 2 + core
+
+    def to_chip(src, dst, send, recv, target):
+        return pltpu.make_async_remote_copy(
+            src_ref=src, dst_ref=dst, send_sem=send, recv_sem=recv,
+            device_id={"patch": target}, device_id_type=MESH,
+        )
+
+    def along(h, source, target, send):
+        where = held.at[h, slot(source)]
+        return to_chip(where, where, send.at[h, source], line_recv.at[h, source], target)
+
+    def aside(h, source):
+        where = held.at[h, slot(source)]
+        return pltpu.make_async_remote_copy(
+            src_ref=where, dst_ref=where, send_sem=side_send.at[h, source],
+            recv_sem=side_recv.at[h, source],
+            device_id={"seq": other_core}, device_id_type=MESH,
+        )
+
+    def lend(h):
+        return to_chip(
+            query.at[h], guest.at[h], guest_send.at[h], guest_recv.at[h], inner
+        )
+
+    def give_back(h):
+        return to_chip(
+            mixed.at[h], returned.at[h], back_send.at[h], back_recv.at[h], outer
+        )
+
+    factor = hd ** (-0.5) * math.log2(math.e)
+    ones = jnp.ones((rows, hd), jnp.bfloat16)
+
+    def attend(rows_q, h):
+        def one(source, total):
+            keys = held[h, source, 0]
+            values = jnp.concatenate([held[h, source, 1], ones], 1)
+            scores = lax.dot_general(
+                rows_q, keys, (((1,), (1,)), ((), ())), preferred_element_type=jnp.float32
+            )
+            weights = jnp.exp2(scores * factor).astype(jnp.bfloat16)
+            return total + jnp.dot(weights, values, preferred_element_type=jnp.float32)
+
+        total = lax.fori_loop(0, 8, one, jnp.zeros((rows, 2 * hd), jnp.float32))
+        return (total[:, :hd] / total[:, hd:]).astype(jnp.bfloat16)
+
+    barrier = pltpu.get_barrier_semaphore()
+    pl.semaphore_signal(barrier, inc=1, device_id={"seq": other_core}, device_id_type=MESH)
+    pl.semaphore_signal(barrier, inc=1, device_id={"patch": inner}, device_id_type=MESH)
+
+    @pl.when(is_mid)
+    def _():
+        pl.semaphore_signal(barrier, inc=1, device_id={"patch": outer}, device_id_type=MESH)
+
+    pl.semaphore_wait(barrier, jnp.where(is_end, 2, 3))
+
+    def arrived(h, source):
+        along(h, source, inner, in_send).wait_recv()
+
+    def siblings(h):
+        def one(source, carry):
+            aside(h, source).wait_recv()
+            return carry
+
+        lax.fori_loop(0, 4, one, 0)
+
+    def store_own(h, carry):
+        held[h, slot(chip)] = pair[h]
+        return carry
+
+    lax.fori_loop(0, heads, store_own, 0)
+
+    @pl.when(is_end)
+    def _():
+        def push(h, carry):
+            along(h, chip, inner, in_send).start()
+
+            @pl.when(h < shared)
+            def _():
+                aside(h, chip).start()
+
+            @pl.when(h >= shared)
+            def _():
+                lend(h).start()
+
+            return carry
+
+        lax.fori_loop(0, heads, push, 0)
+
+        def step(h, carry):
+            for source in (my_mid, far_mid, far_end):
+                arrived(h, source)
+                aside(h, source).start()
+            siblings(h)
+            returned[h] = attend(query[h], h)
+            return carry
+
+        lax.fori_loop(0, shared, step, 0)
+
+        def finish(h, carry):
+            give_back(h).wait_recv()
+            return carry
+
+        lax.fori_loop(shared, heads, finish, 0)
+
+        def drain(h, carry):
+            along(h, chip, inner, in_send).wait_send()
+
+            @pl.when(h < shared)
+            def _():
+                for source in (chip, my_mid, far_mid, far_end):
+                    aside(h, source).wait_send()
+
+            @pl.when(h >= shared)
+            def _():
+                lend(h).wait_send()
+
+            return carry
+
+        lax.fori_loop(0, heads, drain, 0)
+
+    @pl.when(is_mid)
+    def _():
+        def push(h, carry):
+            @pl.when(h < 2)
+            def _():
+                along(h, chip, inner, in_send).start()
+
+            @pl.when(h < shared)
+            def _():
+                along(h, chip, outer, out_send).start()
+
+            aside(h, chip).start()
+            return carry
+
+        lax.fori_loop(0, heads, push, 0)
+
+        def take_end(h):
+            arrived(h, my_end)
+            along(h, my_end, inner, in_send).start()
+            aside(h, my_end).start()
+
+        take_end(0)
+
+        def step(h, carry):
+            @pl.when(h + 2 < heads)
+            def _():
+                along(h + 2, chip, inner, in_send).start()
+
+            @pl.when(h + 1 < heads)
+            def _():
+                take_end(h + 1)
+
+            for source in (far_mid, far_end):
+                arrived(h, source)
+                aside(h, source).start()
+
+                @pl.when(h < shared)
+                def _():
+                    along(h, source, outer, out_send).start()
+
+            siblings(h)
+
+            @pl.when(h >= shared)
+            def _():
+                lend(h).wait_recv()
+                mixed[h] = attend(guest[h], h)
+                give_back(h).start()
+
+            returned[h] = attend(query[h], h)
+            return carry
+
+        lax.fori_loop(0, heads, step, 0)
+
+        def drain(h, carry):
+            along(h, chip, inner, in_send).wait_send()
+            along(h, my_end, inner, in_send).wait_send()
+            for source in (chip, my_end, far_mid, far_end):
+                aside(h, source).wait_send()
+
+            @pl.when(h < shared)
+            def _():
+                for source in (chip, far_mid, far_end):
+                    along(h, source, outer, out_send).wait_send()
+
+            @pl.when(h >= shared)
+            def _():
+                give_back(h).wait_send()
+
+            return carry
+
+        lax.fori_loop(0, heads, drain, 0)
+
+    for h in range(heads):
+        out[:, h * hd : (h + 1) * hd] = returned[h]
+
+
+def attend_call(query, pair):
+    heads, rows, hd = query.shape
+    dma = pltpu.SemaphoreType.DMA
+    vmem = lambda *shape: pltpu.VMEM(shape, jnp.bfloat16)
+    return pl.pallas_call(
+        attend_kernel,
+        out_shape=jax.ShapeDtypeStruct((rows, heads * hd), jnp.bfloat16),
+        in_specs=[pl.BlockSpec(memory_space=pltpu.VMEM)] * 2,
+        out_specs=pl.BlockSpec(memory_space=pltpu.VMEM),
+        scratch_shapes=[
+            vmem(heads, 8, 2, rows, hd),
+            vmem(heads, rows, hd),
+            vmem(heads, rows, hd),
+            vmem(heads, rows, hd),
+        ]
+        + [dma((heads, 4))] * 5
+        + [dma((heads,))] * 4,
+        compiler_params=pltpu.CompilerParams(
+            collective_id=0, has_side_effects=True, vmem_limit_bytes=48 * 2**20
+        ),
+    )(query, pair)
+
+
+def on_device_line(
+    query_raw,
+    key_raw,
+    value_raw,
+    key_cache,
+    value_cache,
+    norm_gain,
+    layout,
+    group_size,
+    step_index,
+    gate_table,
+    out_weight,
+):
+    query_rot, pair, key_mine, value_mine = prepare_call(
+        query_raw, key_raw, value_raw, key_cache, value_cache, norm_gain, layout, group_size
+    )
+    attn_rows = attend_call(query_rot, pair)
+    text_flag = (layout[0] == 0).astype(jnp.bfloat16)
+    pair_attn = lax.all_gather(attn_rows, "seq", axis=0, tiled=True)
+    pair_text = lax.all_gather(text_flag, "seq", axis=0, tiled=True)
+    share = pair_attn.shape[0] // 2
+
+    def both_streams(block, block_text):
+        text_part = jnp.dot(block, out_weight[0], preferred_element_type=jnp.float32)
+        image_part = jnp.dot(block, out_weight[1], preferred_element_type=jnp.float32)
+        return jnp.where(block_text[:, None] > 0, text_part, image_part)
+
+    def image_only(block, block_text):
+        return jnp.dot(block, out_weight[1], preferred_element_type=jnp.float32)
+
+    partial = lax.cond(
+        jnp.any(pair_text > 0), both_streams, image_only, pair_attn, pair_text
+    )
+    mine = lax.axis_index("tensor")
+    kept = lax.dynamic_slice_in_dim(partial, mine * share, share, 0)
+    sent = lax.dynamic_slice_in_dim(partial, (1 - mine) * share, share, 0).astype(jnp.bfloat16)
+    got = lax.ppermute(sent, "tensor", [(0, 1), (1, 0)])
+    projected = kept + got.astype(jnp.float32)
+    mine_text = lax.dynamic_slice_in_dim(pair_text, mine * share, share, 0)
+    chosen = (jnp.arange(gate_table.shape[1]) == step_index[0]).astype(jnp.float32)
+    gates = jnp.sum(gate_table * chosen[None, :, None], 1)
+    gate_rows = jnp.where(mine_text[:, None] > 0, gates[0][None, :], gates[1][None, :])
+    return ((gate_rows * projected).astype(jnp.bfloat16), key_mine, value_mine)
+
+
 def solution(mesh):
     in_specs = (
         P(("group", "patch", "seq"), "tensor"),
@@ -208,6 +622,7 @@
         P(("group", "patch", "seq"), "tensor"),
         P(("group", "patch", "seq"), "tensor"),
     )
+    fast = mesh.shape["patch"] == 4 and mesh.shape["tensor"] == 2 and mesh.shape["seq"] == 2
     return jax.shard_map(
-        on_device, mesh=mesh, in_specs=in_specs, out_specs=out_specs, check_vma=False
-    )
+        on_device_line if fast else on_device, mesh=mesh, in_specs=in_specs, out_specs=out_specs, check_vma=False
+    )

time: 296 us -> 154 us (0.52)
  waiting for transfers between devices: 162 us -> 31.1 us
  Pallas kernels: 0 us -> 81 us
  local copies, waits for them, and re-layouts: 45.8 us -> 9.37 us
  matrix products: 38 us -> 8.27 us
  other arithmetic: 30.7 us -> 4.65 us
    all_gather x3 -> x1, waiting for transfers between devices: 107 us -> 5.62 us  [on_device_line(): pair_attn = lax.all_gather(attn_rows, 'seq', axis=0, tiled=True)]
    pallas_call x0 -> x2, Pallas kernels: none -> 81 us  [the longest x1 74.3 us: attend_call(): pl.pallas_call(attend_kernel, out_shape=jax.ShapeDtypeStruct((rows, heads...]
    reduce_scatter x1 -> x0, waiting for transfers between devices: 54.9 us -> none  [on_device(): lax.psum_scatter(lax.cond(jnp.any(block_text > 0), both_streams, image_on...]
    dot_general x4 -> x0, matrix products: 29.6 us -> none  [the longest x2 16.4 us: one_block(): jnp.einsum('hqk,khd->hqd', weights.astype(jnp.bfloat16), values, preferre...]
    ppermute x0 -> x1, waiting for transfers between devices: none -> 25.5 us  [on_device_line(): got = lax.ppermute(sent, 'tensor', [(0, 1), (1, 0)])]
    concatenate x4 -> x0, local copies, waits for them, and re-layouts: 24.5 us -> none  [the longest x2 17.1 us: partner(): jnp.concatenate([values[..., :plain_dims], -values[..., plain_dims + half...]
    convert_element_type x8 -> x4, other arithmetic: 12 us -> 3.75 us  [the longest x1 3.06 us: on_device_line(): return ((gate_rows * projected).astype(jnp.bfloat16), key_mine, value_mine)]
    mul x4 -> x0, other arithmetic: 6.76 us -> none  [the longest x2 3.57 us: compress(): half_ms = jnp.mean(halves * halves, -1)]
  transfers between devices with their start and end apart: 4 -> 2, of which waited for: 4 -> 2; matrix products, arithmetic and copies ran while one was open for 2% -> 1% of each run, Pallas kernels for 0% -> 0%
where the time goes in v1:
time: 154 us; the launch traced here: 153 us
  Pallas kernels  81 us (53%)
  waiting for transfers between devices  31.1 us (20%)
  between operations  15.4 us (10%)
  local copies, waits for them, and re-layouts  9.37 us (6%)
  matrix products  8.27 us (5%)
  other arithmetic  4.65 us (3%)
  starting transfers between devices  1.83 us (1%)
  blocking collectives  1.78 us (1%)
    pallas_call x1, Pallas kernels, attend_call(): pl.pallas_call(attend_kernel, out_shape=jax.ShapeDtypeStruct((rows, heads...  74.3 us
    ppermute x1, waiting for transfers between devices, on_device_line(): got = lax.ppermute(sent, 'tensor', [(0, 1), (1, 0)])  25.5 us
    unnamed x20, local copies, waits for them, and re-layouts  7.35 us
    pallas_call x1, Pallas kernels, prepare_call(): pl.pallas_call(prepare_kernel, grid=(heads,), in_specs=[pl.BlockSpec(memo...  6.73 us
    all_gather x1, waiting for transfers between devices, on_device_line(): pair_attn = lax.all_gather(attn_rows, 'seq', axis=0, tiled=True)  5.62 us
    dot_general x1, matrix products, both_streams(): jnp.dot(block, out_weight[0], preferred_element_type=jnp.float32)  4.16 us
    dot_general x1, matrix products, both_streams(): jnp.dot(block, out_weight[1], preferred_element_type=jnp.float32)  4.12 us
  transfers between devices with their start and end apart: 2, of which 2 were waited for; matrix products, arithmetic and copies ran while one was open for 1% of the time, Pallas kernels for 0%

profile of v1, /device:TPU:0, one launch (start us, length us, event | category | flops | bytes accessed | tf_op | source)
XLA Modules:
  0.0 153.5 jit_solution(8842375230400600373)
XLA Ops:
  7.2 0.0 all-gather.3.cloned.1.call-start
  7.2 0.7 convert_element_type.32
  7.9 0.1 copy.15
  8.0 0.0 copy-start
  8.1 1.1 copy-done
  9.1 0.0 copy-start.1
  9.1 1.1 copy-done.1
  10.2 0.0 copy-start.2
  10.2 1.1 copy-done.2
  11.2 0.0 copy-start.3
  11.2 1.1 copy-done.3
  12.3 0.0 copy-start.4
  12.3 1.1 copy-done.4
  13.4 0.0 copy-start.5
  13.4 0.7 copy-done.5
  14.1 0.0 copy-start.6
  14.1 0.7 copy-done.6
  14.7 0.0 copy-start.7
  14.7 0.7 copy-done.7
  15.4 0.0 copy-start.11
  15.4 6.7 %shard_map.139 = (bf16[6,384,128]{2,1,0:T(8,128)(2,1)S(1)}, bf16[6,2,384,128]{3,2,1,0:T(8,128)(2,1)S(1)}, bf16[384,768]{1,0:T(8,128)(2,1)}, bf16[384,768]{1,0:T(8,128)(2,1)}) custom-call(s32[6]{0:T(128)S(1)} %copy-done.7, f32[384,2]{1,0:T(8,128)S(1)} %bitcast.16, f32[4,128]{1,0:T(4,128)S(1)} %bitcast.17, f32[8,128]{1,0:T(8,128)S(1)} %copy-done.5, ...), custom_call_target="tpu_custom_call" | custom-call | tf_op jit(solution)/shard_map/pallas_call | solution.py:284
  22.1 74.3 %shard_map.140 = bf16[384,768]{1,0:T(8,128)(2,1)} custom-call(bf16[6,384,128]{2,1,0:T(8,128)(2,1)S(1)} %get-tuple-element.25.query, bf16[6,2,384,128]{3,2,1,0:T(8,128)(2,1)S(1)} %get-tuple-element.26.pair), custom_call_target="tpu_custom_call" | custom-call | tf_op jit(solution)/shard_map/pallas_call | solution.py:542
  96.4 0.0 all-gather.3.cloned.1.call-update
  96.5 0.0 copy-done.11
  96.5 1.8 %all-gather = bf16[1,768]{1,0:T(2,128)(2,1)S(1)} all-gather(bf16[1,384]{1,0:T(2,128)(2,1)S(1)} %compare_convert_fusion), channel_id=2, replica_groups=mesh['group'=2,'patch'=4,'tensor'=2,'seq'=2] {'seq'}, dimensions={1}, use_global_device_ids=true | all-gather | bytes 2304 | tf_op jit(solution)/shard_map/all_gather | solution.py:580
  98.3 0.6 compare_reduce_fusion.1
  99.6 5.6 %all-gather.3.cloned.1.call-done = bf16[768,768]{1,0:T(8,128)(2,1)} async-done(((bf16[384,768]{1,0:T(8,128)(2,1)}), bf16[768,768]{1,0:T(8,128)(2,1)}) %all-gather.3.cloned.1.call-update) | async-done | bytes 1179664 | tf_op jit(solution)/shard_map/all_gather | solution.py:579
  105.2 8.3 %conditional.1 = (f32[768,1536]{1,0:T(8,128)}) conditional(s32[]{:T(128)} %convert_element_type.31, (bf16[2,768,1536]{2,1,0:T(8,128)(2,1)}, bf16[768,768]{1,0:T(8,128)(2,1)}) %tuple.14, (bf16[768]{0:T(1024)(128)(2,1)S(1)}, bf16[2,768,1536]{2,1,0:T(8,128)(2,1)}, bf16[768,768]{1,0:T(8,128)(2,1)}) %tuple.15), branch_computations={%region_2.3_spmd, %region_3.4_spmd} | conditional | flops 3625059072 | bytes 44830016 | solution.py:591
  105.2 0.0 copy-start.8
  105.2 0.0 copy-start.9
  105.2 4.2 %fusion.4 = f32[768,1536]{1,0:T(8,128)S(1)} fusion(bf16[768,768]{1,0:T(8,128)(2,1)} %get-tuple-element.16, bf16[2,768,1536]{2,1,0:T(8,128)(2,1)} %get-tuple-element.17), kind=kOutput, calls=%fused_computation.5 | convolution fusion | flops 1811939328 | bytes 8257536 | tf_op jit(solution)/shard_map/cond/branch_1_fun/dot_general | solution.py:584
  109.4 0.0 copy-done.8
  109.4 0.0 copy-done.9
  109.4 4.1 %convolution_select_fusion = f32[768,1536]{1,0:T(8,128)} fusion(f32[768,1536]{1,0:T(8,128)S(1)} %fusion.4, bf16[768,768]{1,0:T(8,128)(2,1)S(1)} %copy-done.8, bf16[2,768,1536]{2,1,0:T(8,128)(2,1)S(1)} %copy-done.9, pred[768]{0:T(1024)(128)(4,1)S(1)} %broadcast_compare_fusion), kind=kOutput, calls=%fused_computation.3 | convolution fusion | flops 1813118976 | bytes 12977152 | tf_op jit(solution)/shard_map/cond/branch_1_fun/dot_general | solution.py:585
  113.5 0.0 copy-start.10
  113.5 1.8 %dynamic-slice_convert_fusion = bf16[384,1536]{1,0:T(8,128)(2,1)S(1)} fusion(f32[768,1536]{1,0:T(8,128)} %get-tuple-element.31, s32[]{:T(128)S(6)} %select_n.17), kind=kLoop, calls=%fused_computation.11 | loop fusion | bytes 2359300 | tf_op jit(solution)/shard_map/convert_element_type | solution.py:596
  115.4 1.8 %collective-permute-start = (bf16[384,1536]{1,0:T(8,128)(2,1)S(1)}, bf16[384,1536]{1,0:T(8,128)(2,1)S(1)}, u32[]{:S(2)}, u32[]{:S(2)}) collective-permute-start(bf16[384,1536]{1,0:T(8,128)(2,1)S(1)} %dynamic-slice_convert_fusion), channel_id=1, source_target_pairs={{0,2},{2,0},{1,3},{3,1},{4,6},{6,4},{5,7},{7,5},{8,10},{10,8},{9,1... | collective-permute-start | bytes 3538952 | tf_op jit(solution)/shard_map/ppermute | solution.py:597
  117.9 0.0 copy-done.10
  117.9 0.2 multiply_reduce_fusion
  118.1 25.5 %collective-permute-done = bf16[384,1536]{1,0:T(8,128)(2,1)S(1)} collective-permute-done((bf16[384,1536]{1,0:T(8,128)(2,1)S(1)}, bf16[384,1536]{1,0:T(8,128)(2,1)S(1)}, u32[]{:S(2)}, u32[]{:S(2)}) %collective-permute-start) | collective-permute-done | bytes 1179680 | tf_op jit(solution)/shard_map/ppermute | solution.py:597
  143.6 3.1 %multiply_convert_fusion = bf16[384,1536]{1,0:T(8,128)(2,1)} fusion(bf16[384,1536]{1,0:T(8,128)(2,1)S(1)} %collective-permute-done, f32[768,1536]{1,0:T(8,128)} %get-tuple-element.31, s32[]{:T(128)S(6)} %select_n.15, f32[1536]{0:T(1024)S(1)} %get-tuple-element.30, f32[1536]{0:T(1024)S(1)} %get-tuple-element.29, pred[384]{0:T(512)(128)(4,1)S(1)} %compare_reduce_fusion), kind=kLoop, calls=%fused_computation.10 | loop fusion | flops 2949120 | bytes 4731268 | tf_op jit(solution)/shard_map/convert_element_type | solution.py:603
  (6 shorter events, 0.1 us)
Async XLA Ops:
  7.2 98.0 %all-gather.3.cloned.1.call-start = ((), (), s32[]{:S(2)}) async-start(), calls=%async_computation | async-start | bytes 1769472 | tf_op jit(solution)/shard_map/all_gather | solution.py:579
  8.0 1.1 copy-start
  9.1 1.1 copy-start.1
  10.2 1.1 copy-start.2
  11.2 1.1 copy-start.3
  12.3 1.1 copy-start.4
  13.4 0.7 copy-start.5
  14.1 0.7 copy-start.6
  14.7 0.7 copy-start.7
  15.4 81.1 %copy-start.11 = (s32[2,384]{1,0:T(2,128)S(1)}, s32[2,384]{1,0:T(2,128)}, u32[]{:S(2)}) copy-start(s32[2,384]{1,0:T(2,128)} %param.20) | copy-start | bytes 9220
  105.2 4.2 %copy-start.8 = (bf16[768,768]{1,0:T(8,128)(2,1)S(1)}, bf16[768,768]{1,0:T(8,128)(2,1)}, u32[]{:S(2)}) copy-start(bf16[768,768]{1,0:T(8,128)(2,1)} %get-tuple-element.16) | copy-start | bytes 3538948 | tf_op jit(solution)/shard_map/cond
  105.2 4.2 %copy-start.9 = (bf16[2,768,1536]{2,1,0:T(8,128)(2,1)S(1)}, bf16[2,768,1536]{2,1,0:T(8,128)(2,1)}, u32[]{:S(2)}) copy-start(bf16[2,768,1536]{2,1,0:T(8,128)(2,1)} %get-tuple-element.17) | copy-start | bytes 14155780 | tf_op jit(solution)/shard_map/cond
  113.5 4.3 %copy-start.10 = (f32[2,28,1536]{2,0,1:T(2,128)S(1)}, f32[2,28,1536]{2,0,1:T(2,128)}, u32[]{:S(2)}) copy-start(f32[2,28,1536]{2,0,1:T(2,128)} %param.23) | copy-start | bytes 1032196
  115.4 28.2 %collective-permute-start = (bf16[384,1536]{1,0:T(8,128)(2,1)S(1)}, bf16[384,1536]{1,0:T(8,128)(2,1)S(1)}, u32[]{:S(2)}, u32[]{:S(2)}) collective-permute-start(bf16[384,1536]{1,0:T(8,128)(2,1)S(1)} %dynamic-slice_convert_fusion), channel_id=1, source_target_pairs={{0,2},{2,0},{1,3},{3,1},{4,6},{6,4},{5,7},{7,5},{8,10},{10,8},{9,1... | collective-permute-start | bytes 3538952 | tf_op jit(solution)/shard_map/ppermute | solution.py:597
Sparse Core Ops, SparseCore 0:
  96.6 8.5 all-gather.2

commit v2 on v1

--- a/solution.py
+++ b/solution.py
@@ -196,6 +196,8 @@
 
 MESH = pl.DeviceIdType.MESH
 GATHER_SHARE = 2
+CHUNKS = 3
+TEXT_PART = 12
 
 
 def lane_tables(head_dim):
@@ -304,7 +306,7 @@
             jax.ShapeDtypeStruct((rows, width), jnp.bfloat16),
         ],
         scratch_shapes=[pltpu.VMEM((rows, hd), jnp.float32)] * 5,
-        compiler_params=pltpu.CompilerParams(vmem_limit_bytes=32 * 2**20),
+        compiler_params=pltpu.CompilerParams(vmem_limit_bytes=60 * 2**20),
     )(
         group_size,
         layout.astype(jnp.float32).T,
@@ -319,10 +321,14 @@
 
 
 def attend_kernel(
-    query, pair, out, held, guest, mixed, returned, in_send, out_send, side_send, line_recv,
-    side_recv, guest_send, guest_recv, back_send, back_recv,
+    query, pair, gates, weight, out, held, guest, mixed, returned, full, own_weight, far_weight,
+    in_send, out_send, side_send, line_recv, side_recv, guest_send, guest_recv, back_send,
+    back_recv, full_send, full_recv, across_send, across_recv, group_send, group_recv, load_sem,
 ):
     heads, rows, hd = query.shape
+    features, columns = weight.shape[1:]
+    group = lax.axis_index("group")
+    side = lax.axis_index("tensor")
     shared = heads // GATHER_SHARE
     chip = lax.axis_index("patch")
     core = lax.axis_index("seq")
@@ -368,31 +374,107 @@
             mixed.at[h], returned.at[h], back_send.at[h], back_recv.at[h], outer
         )
 
+    has_text = (chip == 0) & (side == 0)
+    gives_text = (chip == 0) & (side == 1)
+    text_rows = rows * 8 // TEXT_PART
+    chunk = features // 2 // CHUNKS
+
+    def weight_rows(owner, c):
+        return pl.ds(pl.multiple_of(owner * (features // 2) + c * chunk, chunk), chunk)
+
+    def across(stream, c):
+        where = weight_rows(group, c)
+        return pltpu.make_async_remote_copy(
+            src_ref=weight.at[stream, where], dst_ref=far_weight.at[stream, where],
+            send_sem=across_send.at[stream, c], recv_sem=across_recv.at[stream, c],
+            device_id={"tensor": 1 - side}, device_id_type=MESH,
+        )
+
+    def pass_on(stream, c):
+        where = far_weight.at[stream, weight_rows(group, c)]
+        return pltpu.make_async_remote_copy(
+            src_ref=where, dst_ref=where,
+            send_sem=group_send.at[stream, c], recv_sem=group_recv.at[stream, c],
+            device_id={"group": 1 - group}, device_id_type=MESH,
+        )
+
+    def relay(stream, c):
+        across(stream, c).wait_recv()
+        pass_on(stream, c).start()
+
+    def load(stream):
+        return pltpu.make_async_copy(
+            weight.at[stream], own_weight.at[stream], load_sem.at[stream]
+        )
+
+    def hand_over(h, which):
+        if which == 2:
+            target = {"seq": other_core}
+        else:
+            target = {"tensor": 1 - side, "seq": core if which == 0 else other_core}
+        return pltpu.make_async_remote_copy(
+            src_ref=returned.at[h], dst_ref=full.at[side, h],
+            send_sem=full_send.at[min(which, 1), h], recv_sem=full_recv.at[side, h],
+            device_id=target, device_id_type=MESH,
+        )
+
+    def received(origin, h):
+        where = full.at[origin, h]
+        return pltpu.make_async_remote_copy(
+            src_ref=where, dst_ref=where,
+            send_sem=full_send.at[0, h], recv_sem=full_recv.at[origin, h],
+            device_id={"seq": other_core}, device_id_type=MESH,
+        )
+
+    straight = side == core
+
+    def distribute(h):
+        @pl.when(straight)
+        def _():
+            hand_over(h, 2).start()
+            full[side, h] = returned[h]
+
+        @pl.when(jnp.logical_not(straight))
+        def _():
+            hand_over(h, 0).start()
+            hand_over(h, 1).start()
+
     factor = hd ** (-0.5) * math.log2(math.e)
-    ones = jnp.ones((rows, hd), jnp.bfloat16)
 
     def attend(rows_q, h):
-        def one(source, total):
-            keys = held[h, source, 0]
-            values = jnp.concatenate([held[h, source, 1], ones], 1)
+        keys = held[h, :, 0].reshape(8 * rows, hd)
+        values = held[h, :, 1].reshape(8 * rows, hd)
+        values = jnp.concatenate([values, jnp.ones_like(values)], 1)
+        half = rows // 2
+        parts = []
+        for start in (0, half):
             scores = lax.dot_general(
-                rows_q, keys, (((1,), (1,)), ((), ())), preferred_element_type=jnp.float32
+                rows_q[h, start : start + half],
+                keys,
+                (((1,), (1,)), ((), ())),
+                preferred_element_type=jnp.float32,
             )
             weights = jnp.exp2(scores * factor).astype(jnp.bfloat16)
-            return total + jnp.dot(weights, values, preferred_element_type=jnp.float32)
-
-        total = lax.fori_loop(0, 8, one, jnp.zeros((rows, 2 * hd), jnp.float32))
-        return (total[:, :hd] / total[:, hd:]).astype(jnp.bfloat16)
+            total = jnp.dot(weights, values, preferred_element_type=jnp.float32)
+            parts.append((total[:, :hd] / total[:, hd:]).astype(jnp.bfloat16))
+        return jnp.concatenate(parts, 0)
 
     barrier = pltpu.get_barrier_semaphore()
     pl.semaphore_signal(barrier, inc=1, device_id={"seq": other_core}, device_id_type=MESH)
     pl.semaphore_signal(barrier, inc=1, device_id={"patch": inner}, device_id_type=MESH)
 
+    for target in (
+        {"group": 1 - group},
+        {"tensor": 1 - side},
+        {"tensor": 1 - side, "seq": other_core},
+    ):
+        pl.semaphore_signal(barrier, inc=1, device_id=target, device_id_type=MESH)
+
     @pl.when(is_mid)
     def _():
         pl.semaphore_signal(barrier, inc=1, device_id={"patch": outer}, device_id_type=MESH)
 
-    pl.semaphore_wait(barrier, jnp.where(is_end, 2, 3))
+    pl.semaphore_wait(barrier, jnp.where(is_end, 5, 6))
 
     def arrived(h, source):
         along(h, source, inner, in_send).wait_recv()
@@ -410,6 +492,21 @@
 
     lax.fori_loop(0, heads, store_own, 0)
 
+    def start_weights():
+        for c in range(CHUNKS):
+            across(1, c).start()
+
+        @pl.when(gives_text)
+        def _():
+            for c in range(CHUNKS):
+                across(0, c).start()
+
+        load(1).start()
+
+        @pl.when(has_text)
+        def _():
+            load(0).start()
+
     @pl.when(is_end)
     def _():
         def push(h, carry):
@@ -426,19 +523,28 @@
             return carry
 
         lax.fori_loop(0, heads, push, 0)
+        start_weights()
 
         def step(h, carry):
             for source in (my_mid, far_mid, far_end):
                 arrived(h, source)
                 aside(h, source).start()
             siblings(h)
-            returned[h] = attend(query[h], h)
+            returned[h] = attend(query, h)
+            distribute(h)
+            relay(1, h)
             return carry
 
         lax.fori_loop(0, shared, step, 0)
 
         def finish(h, carry):
             give_back(h).wait_recv()
+            distribute(h)
+
+            @pl.when(has_text)
+            def _():
+                relay(0, h - shared)
+
             return carry
 
         lax.fori_loop(shared, heads, finish, 0)
@@ -480,6 +586,7 @@
             along(h, my_end, inner, in_send).start()
             aside(h, my_end).start()
 
+        start_weights()
         take_end(0)
 
         def step(h, carry):
@@ -504,10 +611,16 @@
             @pl.when(h >= shared)
             def _():
                 lend(h).wait_recv()
-                mixed[h] = attend(guest[h], h)
+                mixed[h] = attend(guest, h)
                 give_back(h).start()
 
-            returned[h] = attend(query[h], h)
+            returned[h] = attend(query, h)
+            distribute(h)
+
+            @pl.when(h < CHUNKS)
+            def _():
+                relay(1, h)
+
             return carry
 
         lax.fori_loop(0, heads, step, 0)
@@ -531,31 +644,110 @@
 
         lax.fori_loop(0, heads, drain, 0)
 
-    for h in range(heads):
-        out[:, h * hd : (h + 1) * hd] = returned[h]
-
-
-def attend_call(query, pair):
+    load(1).wait()
+    for c in range(CHUNKS):
+        pass_on(1, c).wait_recv()
+
+    @pl.when(has_text)
+    def _():
+        load(0).wait()
+        for c in range(CHUNKS):
+            pass_on(0, c).wait_recv()
+
+    def collect(h, carry):
+        received(1 - side, h).wait_recv()
+
+        @pl.when(jnp.logical_not(straight))
+        def _():
+            received(side, h).wait_recv()
+
+        return carry
+
+    lax.fori_loop(0, heads, collect, 0)
+    own_rows = jnp.concatenate([full[side, h] for h in range(heads)], 1)
+    far_rows = jnp.concatenate([full[1 - side, h] for h in range(heads)], 1)
+    width = 512
+
+    def project(first, last, stream, place):
+        sums = jnp.dot(
+            own_rows[first:last], own_weight[stream, :, place], preferred_element_type=jnp.float32
+        ) + jnp.dot(
+            far_rows[first:last], far_weight[stream, :, place], preferred_element_type=jnp.float32
+        )
+        out[first:last, place] = (sums * gates[stream : stream + 1, place]).astype(out.dtype)
+
+    def block(index, carry):
+        place = pl.ds(pl.multiple_of(index * width, width), width)
+
+        @pl.when(has_text)
+        def _():
+            project(0, text_rows, 0, place)
+            project(text_rows, rows, 1, place)
+
+        @pl.when(jnp.logical_not(has_text))
+        def _():
+            project(0, rows, 1, place)
+
+        return carry
+
+    lax.fori_loop(0, columns // width, block, 0)
+
+    def drain_rows(h, carry):
+        @pl.when(straight)
+        def _():
+            hand_over(h, 2).wait_send()
+
+        @pl.when(jnp.logical_not(straight))
+        def _():
+            hand_over(h, 0).wait_send()
+            hand_over(h, 1).wait_send()
+
+        return carry
+
+    lax.fori_loop(0, heads, drain_rows, 0)
+    for c in range(CHUNKS):
+        across(1, c).wait_send()
+        pass_on(1, c).wait_send()
+
+    @pl.when(gives_text)
+    def _():
+        for c in range(CHUNKS):
+            across(0, c).wait_send()
+
+    @pl.when(has_text)
+    def _():
+        for c in range(CHUNKS):
+            pass_on(0, c).wait_send()
+
+
+def attend_call(query, pair, gates, weight):
     heads, rows, hd = query.shape
     dma = pltpu.SemaphoreType.DMA
     vmem = lambda *shape: pltpu.VMEM(shape, jnp.bfloat16)
     return pl.pallas_call(
         attend_kernel,
-        out_shape=jax.ShapeDtypeStruct((rows, heads * hd), jnp.bfloat16),
-        in_specs=[pl.BlockSpec(memory_space=pltpu.VMEM)] * 2,
+        out_shape=jax.ShapeDtypeStruct((rows, weight.shape[2]), jnp.bfloat16),
+        in_specs=[pl.BlockSpec(memory_space=pltpu.VMEM)] * 3
+        + [pl.BlockSpec(memory_space=pl.ANY)],
         out_specs=pl.BlockSpec(memory_space=pltpu.VMEM),
         scratch_shapes=[
             vmem(heads, 8, 2, rows, hd),
             vmem(heads, rows, hd),
             vmem(heads, rows, hd),
             vmem(heads, rows, hd),
+            vmem(2, heads, rows, hd),
+            vmem(*weight.shape),
+            vmem(*weight.shape),
         ]
         + [dma((heads, 4))] * 5
-        + [dma((heads,))] * 4,
+        + [dma((heads,))] * 4
+        + [dma((2, heads))] * 2
+        + [dma((2, CHUNKS))] * 4
+        + [dma((2,))],
         compiler_params=pltpu.CompilerParams(
-            collective_id=0, has_side_effects=True, vmem_limit_bytes=48 * 2**20
+            collective_id=0, has_side_effects=True, vmem_limit_bytes=60 * 2**20
         ),
-    )(query, pair)
+    )(query, pair, gates, weight)
 
 
 def on_device_line(
@@ -574,33 +766,9 @@
     query_rot, pair, key_mine, value_mine = prepare_call(
         query_raw, key_raw, value_raw, key_cache, value_cache, norm_gain, layout, group_size
     )
-    attn_rows = attend_call(query_rot, pair)
-    text_flag = (layout[0] == 0).astype(jnp.bfloat16)
-    pair_attn = lax.all_gather(attn_rows, "seq", axis=0, tiled=True)
-    pair_text = lax.all_gather(text_flag, "seq", axis=0, tiled=True)
-    share = pair_attn.shape[0] // 2
-
-    def both_streams(block, block_text):
-        text_part = jnp.dot(block, out_weight[0], preferred_element_type=jnp.float32)
-        image_part = jnp.dot(block, out_weight[1], preferred_element_type=jnp.float32)
-        return jnp.where(block_text[:, None] > 0, text_part, image_part)
-
-    def image_only(block, block_text):
-        return jnp.dot(block, out_weight[1], preferred_element_type=jnp.float32)
-
-    partial = lax.cond(
-        jnp.any(pair_text > 0), both_streams, image_only, pair_attn, pair_text
-    )
-    mine = lax.axis_index("tensor")
-    kept = lax.dynamic_slice_in_dim(partial, mine * share, share, 0)
-    sent = lax.dynamic_slice_in_dim(partial, (1 - mine) * share, share, 0).astype(jnp.bfloat16)
-    got = lax.ppermute(sent, "tensor", [(0, 1), (1, 0)])
-    projected = kept + got.astype(jnp.float32)
-    mine_text = lax.dynamic_slice_in_dim(pair_text, mine * share, share, 0)
     chosen = (jnp.arange(gate_table.shape[1]) == step_index[0]).astype(jnp.float32)
     gates = jnp.sum(gate_table * chosen[None, :, None], 1)
-    gate_rows = jnp.where(mine_text[:, None] > 0, gates[0][None, :], gates[1][None, :])
-    return ((gate_rows * projected).astype(jnp.bfloat16), key_mine, value_mine)
+    return (attend_call(query_rot, pair, gates, out_weight), key_mine, value_mine)
 
 
 def solution(mesh):

time: 154 us -> 104 us (0.68)
  waiting for transfers between devices: 31.1 us -> 0 us
  Pallas kernels: 81 us -> 97.1 us
  between operations: 15.4 us -> 1.3 us
  matrix products: 8.27 us -> 0 us
  local copies, waits for them, and re-layouts: 9.37 us -> 3.18 us
  other arithmetic: 4.65 us -> 2.48 us
  starting transfers between devices: 1.83 us -> 0 us
  blocking collectives: 1.78 us -> 0 us
    ppermute x1 -> x0, waiting for transfers between devices: 25.5 us -> none  [on_device_line(): got = lax.ppermute(sent, 'tensor', [(0, 1), (1, 0)])]
    pallas_call x1, Pallas kernels: 74.3 us -> 89 us  [attend_call(): pl.pallas_call(attend_kernel, out_shape=jax.ShapeDtypeStruct((rows, weigh...]
    dot_general x2 -> x0, matrix products: 8.27 us -> none  [the longest x1 4.16 us: both_streams(): jnp.dot(block, out_weight[0], preferred_element_type=jnp.float32)]
    all_gather x1 -> x0, waiting for transfers between devices: 5.62 us -> none  [on_device_line(): pair_attn = lax.all_gather(attn_rows, 'seq', axis=0, tiled=True)]
    unnamed x20 -> x1, local copies, waits for them, and re-layouts: 7.35 us -> 2.36 us
    convert_element_type x2 -> x0, other arithmetic: 3.06 us -> none  [the longest x1 3.06 us: on_device_line(): return ((gate_rows * projected).astype(jnp.bfloat16), key_mine, value_mine)]
    convert_element_type x1 -> x0, local copies, waits for them, and re-layouts: 1.84 us -> none  [on_device_line(): lax.dynamic_slice_in_dim(partial, (1 - mine) * share, share, 0)]
    ppermute x1 -> x0, starting transfers between devices: 1.79 us -> none  [on_device_line(): got = lax.ppermute(sent, 'tensor', [(0, 1), (1, 0)])]
  transfers between devices with their start and end apart: 2 -> 0, of which waited for: 2 -> 0; matrix products, arithmetic and copies ran while one was open for 1% -> 0% of each run, Pallas kernels for 0% -> 0%
where the time goes in v2:
time: 104 us
  Pallas kernels  97.1 us (93%)
  local copies, waits for them, and re-layouts  3.18 us (3%)
  other arithmetic  2.48 us (2%)
  between operations  1.3 us (1%)
    pallas_call x1, Pallas kernels, attend_call(): pl.pallas_call(attend_kernel, out_shape=jax.ShapeDtypeStruct((rows, weigh...  89 us
    pallas_call x1, Pallas kernels, prepare_call(): pl.pallas_call(prepare_kernel, grid=(heads,), in_specs=[pl.BlockSpec(memo...  8.09 us
    unnamed x1, local copies, waits for them, and re-layouts  2.36 us

profile of v2, /device:TPU:0, one launch (start us, length us, event | category | flops | bytes accessed | tf_op | source)
XLA Modules:
  0.0 104.0 jit_solution(718559658475203011)
XLA Ops:
  1.3 0.7 convert_element_type.10
  2.0 1.8 %multiply_reduce_fusion.gates = f32[2,1536]{1,0:T(2,128)} fusion(f32[2,28,1536]{2,0,1:T(2,128)} %param.21, f32[28]{0:T(128)S(1)} %compare_convert_fusion), kind=kLoop, calls=%fused_computation | loop fusion | flops 168960 | bytes 356464 | tf_op jit(solution)/shard_map/reduce_sum | solution.py:770
  3.8 0.8 copy.15
  4.6 8.1 %shard_map.139 = (bf16[6,384,128]{2,1,0:T(8,128)(2,1)}, bf16[6,2,384,128]{3,2,1,0:T(8,128)(2,1)}, bf16[384,768]{1,0:T(8,128)(2,1)}, bf16[384,768]{1,0:T(8,128)(2,1)}) custom-call(s32[6]{0:T(128)} %sizes.1, f32[384,2]{1,0:T(8,128)} %bitcast.4, f32[4,128]{1,0:T(4,128)} %bitcast.5, f32[8,128]{1,0:T(8,128)} %constant.4.clone.table, bf16[384,768]{1,0:T(8,128)(2,1)} %query.1, ...), custom_call_target="tpu_custom_call" | custom-call | tf_op jit(solution)/shard_map/pallas_call | solution.py:286
  12.7 89.0 %shard_map.140 = bf16[384,1536]{1,0:T(8,128)(2,1)} custom-call(bf16[6,384,128]{2,1,0:T(8,128)(2,1)} %get-tuple-element.7.query, bf16[6,2,384,128]{3,2,1,0:T(8,128)(2,1)} %get-tuple-element.8.pair, f32[2,1536]{1,0:T(2,128)} %multiply_reduce_fusion.gates, bf16[2,768,1536]{2,1,0:T(8,128)(2,1)} %weight.1), custom_call_target="tpu_custom_call" | custom-call | tf_op jit(solution)/shard_map/pallas_call | solution.py:727
  101.6 2.4 %copy.18 = bf16[384,1536]{1,0:T(8,128)(2,1)} copy(bf16[384,1536]{1,0:T(8,128)(2,1)} %shard_map.140) | data formatting | bytes 2359296
  (1 shorter events, 0.0 us)

commit v3 on v2

--- a/solution.py
+++ b/solution.py
@@ -196,7 +196,7 @@
 
 MESH = pl.DeviceIdType.MESH
 GATHER_SHARE = 2
-CHUNKS = 3
+CHUNKS = 6
 TEXT_PART = 12
 
 
@@ -486,20 +486,14 @@
 
         lax.fori_loop(0, 4, one, 0)
 
-    def store_own(h, carry):
-        held[h, slot(chip)] = pair[h]
-        return carry
-
-    lax.fori_loop(0, heads, store_own, 0)
-
     def start_weights():
+        @pl.when(gives_text)
+        def _():
+            for c in range(CHUNKS):
+                across(0, c).start()
+
         for c in range(CHUNKS):
             across(1, c).start()
-
-        @pl.when(gives_text)
-        def _():
-            for c in range(CHUNKS):
-                across(0, c).start()
 
         load(1).start()
 
@@ -510,6 +504,7 @@
     @pl.when(is_end)
     def _():
         def push(h, carry):
+            held[h, slot(chip)] = pair[h]
             along(h, chip, inner, in_send).start()
 
             @pl.when(h < shared)
@@ -532,19 +527,21 @@
             siblings(h)
             returned[h] = attend(query, h)
             distribute(h)
-            relay(1, h)
+
+            @pl.when(has_text)
+            def _():
+                for c in range(2):
+                    relay(0, 2 * h + c)
+
             return carry
 
         lax.fori_loop(0, shared, step, 0)
 
         def finish(h, carry):
+            for c in range(2):
+                relay(1, 2 * (h - shared) + c)
             give_back(h).wait_recv()
             distribute(h)
-
-            @pl.when(has_text)
-            def _():
-                relay(0, h - shared)
-
             return carry
 
         lax.fori_loop(shared, heads, finish, 0)
@@ -568,6 +565,7 @@
     @pl.when(is_mid)
     def _():
         def push(h, carry):
+            held[h, slot(chip)] = pair[h]
             @pl.when(h < 2)
             def _():
                 along(h, chip, inner, in_send).start()
@@ -617,10 +615,7 @@
             returned[h] = attend(query, h)
             distribute(h)
 
-            @pl.when(h < CHUNKS)
-            def _():
-                relay(1, h)
-
+            relay(1, h)
             return carry
 
         lax.fori_loop(0, heads, step, 0)

time: 104 us -> 105 us (level)
  no operation moved by 1% of the time
where the time goes in v3:
time: 105 us; the launch traced here: 104 us
  Pallas kernels  97.3 us (93%)
  local copies, waits for them, and re-layouts  3.18 us (3%)
  other arithmetic  2.48 us (2%)
  between operations  1.3 us (1%)
    pallas_call x1, Pallas kernels, attend_call(): pl.pallas_call(attend_kernel, out_shape=jax.ShapeDtypeStruct((rows, weigh...  89.2 us
    pallas_call x1, Pallas kernels, prepare_call(): pl.pallas_call(prepare_kernel, grid=(heads,), in_specs=[pl.BlockSpec(memo...  8.09 us
    unnamed x1, local copies, waits for them, and re-layouts  2.36 us

profile of v3, /device:TPU:0, one launch (start us, length us, event | category | flops | bytes accessed | tf_op | source)
XLA Modules:
  0.0 104.2 jit_solution(11444412342878195707)
XLA Ops:
  1.3 0.7 convert_element_type.10
  2.0 1.8 %multiply_reduce_fusion.gates = f32[2,1536]{1,0:T(2,128)} fusion(f32[2,28,1536]{2,0,1:T(2,128)} %param.21, f32[28]{0:T(128)S(1)} %compare_convert_fusion), kind=kLoop, calls=%fused_computation | loop fusion | flops 168960 | bytes 356464 | tf_op jit(solution)/shard_map/reduce_sum | solution.py:765
  3.8 0.8 copy.15
  4.6 8.1 %shard_map.139 = (bf16[6,384,128]{2,1,0:T(8,128)(2,1)}, bf16[6,2,384,128]{3,2,1,0:T(8,128)(2,1)}, bf16[384,768]{1,0:T(8,128)(2,1)}, bf16[384,768]{1,0:T(8,128)(2,1)}) custom-call(s32[6]{0:T(128)} %sizes.1, f32[384,2]{1,0:T(8,128)} %bitcast.4, f32[4,128]{1,0:T(4,128)} %bitcast.5, f32[8,128]{1,0:T(8,128)} %constant.4.clone.table, bf16[384,768]{1,0:T(8,128)(2,1)} %query.1, ...), custom_call_target="tpu_custom_call" | custom-call | tf_op jit(solution)/shard_map/pallas_call | solution.py:286
  12.7 89.2 %shard_map.140 = bf16[384,1536]{1,0:T(8,128)(2,1)} custom-call(bf16[6,384,128]{2,1,0:T(8,128)(2,1)} %get-tuple-element.7.query, bf16[6,2,384,128]{3,2,1,0:T(8,128)(2,1)} %get-tuple-element.8.pair, f32[2,1536]{1,0:T(2,128)} %multiply_reduce_fusion.gates, bf16[2,768,1536]{2,1,0:T(8,128)(2,1)} %weight.1), custom_call_target="tpu_custom_call" | custom-call | tf_op jit(solution)/shard_map/pallas_call | solution.py:722
  101.9 2.4 %copy.18 = bf16[384,1536]{1,0:T(8,128)(2,1)} copy(bf16[384,1536]{1,0:T(8,128)(2,1)} %shard_map.140) | data formatting | bytes 2359296
  (1 shorter events, 0.0 us)

commit v4 on v2

--- a/solution.py
+++ b/solution.py
@@ -223,105 +223,10 @@
     )
 
 
-def prepare_kernel(
-    sizes, positions, gains, table, query, key, value, key_old, value_old,
-    query_out, pair_out, key_out, value_out, cosine, sine_low, sine_high, gain_q, gain_k,
-):
-    head = pl.program_id(0)
-    head_dim = query.shape[1]
-    half_len = RB // 2
-
-    @pl.when(head == 0)
-    def _():
-        rows_id = positions[:, 0:1]
-        angle = rows_id * table[0:1, :] + positions[:, 1:2] * table[1:2, :]
-        sine = jnp.sin(angle)
-        cosine[...] = jnp.cos(angle)
-        sine_low[...] = sine * table[2:3, :]
-        sine_high[...] = sine * table[3:4, :]
-        text = rows_id == 0
-        gain_q[...] = jnp.where(text, gains[0:1, :], gains[2:3, :])
-        gain_k[...] = jnp.where(text, gains[1:2, :], gains[3:4, :])
-
-    full = jnp.full((head_dim, head_dim), 1.0 / head_dim, jnp.float32)
-    row = lax.broadcasted_iota(jnp.int32, (head_dim, head_dim), 0) < head_dim // 2
-    col = lax.broadcasted_iota(jnp.int32, (head_dim, head_dim), 1) < head_dim // 2
-    halves = jnp.where(row == col, 2.0 / head_dim, 0.0)
-    whole = (sizes[head] == head_dim).astype(jnp.float32)
-    grouped = (whole * full + (1.0 - whole) * halves).astype(jnp.bfloat16)
-    full = full.astype(jnp.bfloat16)
-
-    def embed(raw, gain):
-        values = raw[...].astype(jnp.float32)
-        normed = values * lax.rsqrt(split_dot(values * values, full) + norm_eps) * gain[...]
-        return (
-            normed * cosine[...]
-            + pltpu.roll(normed, head_dim - half_len, 1) * sine_low[...]
-            + pltpu.roll(normed, half_len, 1) * sine_high[...]
-        )
-
-    def update(fresh, old):
-        kept = old[...].astype(jnp.float32)
-        residual = fresh - kept
-        scale = jnp.sqrt(split_dot(residual * residual, grouped) + norm_eps)
-        scale = scale.astype(jnp.bfloat16).astype(jnp.float32)
-        code = jnp.tanh(residual / scale).astype(jnp.bfloat16).astype(jnp.float32)
-        return (kept + scale * code).astype(jnp.bfloat16)
-
-    query_out[0] = embed(query, gain_q).astype(jnp.bfloat16)
-    key_next = update(embed(key, gain_k), key_old)
-    value_next = update(value[...].astype(jnp.float32), value_old)
-    pair_out[0, 0] = key_next
-    pair_out[0, 1] = value_next
-    key_out[...] = key_next
-    value_out[...] = value_next
-
-
-def prepare_call(query, key, value, key_old, value_old, norm_gain, layout, group_size):
-    rows, width = query.shape
-    heads = group_size.shape[0]
-    hd = width // heads
-    block = pl.BlockSpec((rows, hd), lambda h: (0, h))
-    whole = lambda *shape: pl.BlockSpec(shape, lambda h: (0,) * len(shape))
-    return pl.pallas_call(
-        prepare_kernel,
-        grid=(heads,),
-        in_specs=[
-            pl.BlockSpec(memory_space=pltpu.SMEM),
-            whole(rows, 2),
-            whole(4, hd),
-            whole(8, hd),
-        ]
-        + [block] * 5,
-        out_specs=[
-            pl.BlockSpec((1, rows, hd), lambda h: (h, 0, 0)),
-            pl.BlockSpec((1, 2, rows, hd), lambda h: (h, 0, 0, 0)),
-            block,
-            block,
-        ],
-        out_shape=[
-            jax.ShapeDtypeStruct((heads, rows, hd), jnp.bfloat16),
-            jax.ShapeDtypeStruct((heads, 2, rows, hd), jnp.bfloat16),
-            jax.ShapeDtypeStruct((rows, width), jnp.bfloat16),
-            jax.ShapeDtypeStruct((rows, width), jnp.bfloat16),
-        ],
-        scratch_shapes=[pltpu.VMEM((rows, hd), jnp.float32)] * 5,
-        compiler_params=pltpu.CompilerParams(vmem_limit_bytes=60 * 2**20),
-    )(
-        group_size,
-        layout.astype(jnp.float32).T,
-        norm_gain.reshape(4, hd),
-        lane_tables(hd),
-        query,
-        key,
-        value,
-        key_old,
-        value_old,
-    )
-
-
 def attend_kernel(
-    query, pair, gates, weight, out, held, guest, mixed, returned, full, own_weight, far_weight,
+    sizes, step_index, positions, gains, table, query_raw, key_raw, value_raw, key_old, value_old,
+    gate_table, weight, out, key_out, value_out, query, gates, cosine, sine_low, sine_high,
+    gain_q, gain_k, held, guest, mixed, returned, full, own_weight, far_weight,
     in_send, out_send, side_send, line_recv, side_recv, guest_send, guest_recv, back_send,
     back_recv, full_send, full_recv, across_send, across_recv, group_send, group_recv, load_sem,
 ):
@@ -474,6 +379,55 @@
     def _():
         pl.semaphore_signal(barrier, inc=1, device_id={"patch": outer}, device_id_type=MESH)
 
+    row_ids = positions[:, 0:1]
+    angle = row_ids * table[0:1, :] + positions[:, 1:2] * table[1:2, :]
+    sine = jnp.sin(angle)
+    cosine[...] = jnp.cos(angle)
+    sine_low[...] = sine * table[2:3, :]
+    sine_high[...] = sine * table[3:4, :]
+    text = row_ids == 0
+    gain_q[...] = jnp.where(text, gains[0:1, :], gains[2:3, :])
+    gain_k[...] = jnp.where(text, gains[1:2, :], gains[3:4, :])
+    for stream in range(2):
+        gates[stream : stream + 1, :] = gate_table[stream, pl.ds(step_index[0], 1), :]
+
+    full_mean = jnp.full((hd, hd), 1.0 / hd, jnp.float32)
+    in_low = lax.broadcasted_iota(jnp.int32, (hd, hd), 0) < hd // 2
+    out_low = lax.broadcasted_iota(jnp.int32, (hd, hd), 1) < hd // 2
+    half_mean = jnp.where(in_low == out_low, 2.0 / hd, 0.0)
+    half_len = RB // 2
+
+    def prepare_head(h):
+        place = pl.ds(pl.multiple_of(h * hd, hd), hd)
+        whole = (sizes[h] == hd).astype(jnp.float32)
+        grouped = (whole * full_mean + (1.0 - whole) * half_mean).astype(jnp.bfloat16)
+
+        def embed(raw, gain):
+            values = raw[:, place].astype(jnp.float32)
+            mean_sq = split_dot(values * values, full_mean.astype(jnp.bfloat16))
+            normed = values * lax.rsqrt(mean_sq + norm_eps) * gain[...]
+            return (
+                normed * cosine[...]
+                + pltpu.roll(normed, hd - half_len, 1) * sine_low[...]
+                + pltpu.roll(normed, half_len, 1) * sine_high[...]
+            )
+
+        def update(fresh, old):
+            kept = old[:, place].astype(jnp.float32)
+            residual = fresh - kept
+            scale = jnp.sqrt(split_dot(residual * residual, grouped) + norm_eps)
+            scale = scale.astype(jnp.bfloat16).astype(jnp.float32)
+            code = jnp.tanh(residual / scale).astype(jnp.bfloat16).astype(jnp.float32)
+            return (kept + scale * code).astype(jnp.bfloat16)
+
+        key_next = update(embed(key_raw, gain_k), key_old)
+        value_next = update(value_raw[:, place].astype(jnp.float32), value_old)
+        held[h, slot(chip), 0] = key_next
+        held[h, slot(chip), 1] = value_next
+        key_out[:, place] = key_next
+        value_out[:, place] = value_next
+        query[h] = embed(query_raw, gain_q).astype(jnp.bfloat16)
+
     pl.semaphore_wait(barrier, jnp.where(is_end, 5, 6))
 
     def arrived(h, source):
@@ -486,20 +440,16 @@
 
         lax.fori_loop(0, 4, one, 0)
 
-    def store_own(h, carry):
-        held[h, slot(chip)] = pair[h]
-        return carry
-
-    lax.fori_loop(0, heads, store_own, 0)
-
     def start_weights():
-        for c in range(CHUNKS):
-            across(1, c).start()
-
         @pl.when(gives_text)
         def _():
+            across(0, 0).start()
+            across(0, 1).start()
+
+        @pl.when(jnp.logical_not(gives_text))
+        def _():
             for c in range(CHUNKS):
-                across(0, c).start()
+                across(1, c).start()
 
         load(1).start()
 
@@ -510,6 +460,7 @@
     @pl.when(is_end)
     def _():
         def push(h, carry):
+            prepare_head(h)
             along(h, chip, inner, in_send).start()
 
             @pl.when(h < shared)
@@ -532,19 +483,43 @@
             siblings(h)
             returned[h] = attend(query, h)
             distribute(h)
-            relay(1, h)
+
+            @pl.when(has_text)
+            def _():
+                relay(0, h)
+
+            @pl.when(jnp.logical_not(has_text))
+            def _():
+                relay(1, h)
+
+            @pl.when(gives_text)
+            def _():
+                across(0, h).wait_send()
+
+                @pl.when(h == 0)
+                def _():
+                    across(0, 2).start()
+
+                @pl.when(h > 0)
+                def _():
+                    across(1, h - 1).start()
+
             return carry
 
         lax.fori_loop(0, shared, step, 0)
 
         def finish(h, carry):
+            @pl.when(has_text)
+            def _():
+                relay(1, h - shared)
+
+            @pl.when(gives_text & (h == shared))
+            def _():
+                across(1, 0).wait_send()
+                across(1, 2).start()
+
             give_back(h).wait_recv()
             distribute(h)
-
-            @pl.when(has_text)
-            def _():
-                relay(0, h - shared)
-
             return carry
 
         lax.fori_loop(shared, heads, finish, 0)
@@ -568,6 +543,7 @@
     @pl.when(is_mid)
     def _():
         def push(h, carry):
+            prepare_head(h)
             @pl.when(h < 2)
             def _():
                 along(h, chip, inner, in_send).start()
@@ -706,48 +682,18 @@
 
     lax.fori_loop(0, heads, drain_rows, 0)
     for c in range(CHUNKS):
+        pass_on(1, c).wait_send()
+    for c in range(1, CHUNKS):
         across(1, c).wait_send()
-        pass_on(1, c).wait_send()
-
-    @pl.when(gives_text)
+
+    @pl.when(jnp.logical_not(gives_text))
     def _():
-        for c in range(CHUNKS):
-            across(0, c).wait_send()
+        across(1, 0).wait_send()
 
     @pl.when(has_text)
     def _():
         for c in range(CHUNKS):
             pass_on(0, c).wait_send()
-
-
-def attend_call(query, pair, gates, weight):
-    heads, rows, hd = query.shape
-    dma = pltpu.SemaphoreType.DMA
-    vmem = lambda *shape: pltpu.VMEM(shape, jnp.bfloat16)
-    return pl.pallas_call(
-        attend_kernel,
-        out_shape=jax.ShapeDtypeStruct((rows, weight.shape[2]), jnp.bfloat16),
-        in_specs=[pl.BlockSpec(memory_space=pltpu.VMEM)] * 3
-        + [pl.BlockSpec(memory_space=pl.ANY)],
-        out_specs=pl.BlockSpec(memory_space=pltpu.VMEM),
-        scratch_shapes=[
-            vmem(heads, 8, 2, rows, hd),
-            vmem(heads, rows, hd),
-            vmem(heads, rows, hd),
-            vmem(heads, rows, hd),
-            vmem(2, heads, rows, hd),
-            vmem(*weight.shape),
-            vmem(*weight.shape),
-        ]
-        + [dma((heads, 4))] * 5
-        + [dma((heads,))] * 4
-        + [dma((2, heads))] * 2
-        + [dma((2, CHUNKS))] * 4
-        + [dma((2,))],
-        compiler_params=pltpu.CompilerParams(
-            collective_id=0, has_side_effects=True, vmem_limit_bytes=60 * 2**20
-        ),
-    )(query, pair, gates, weight)
 
 
 def on_device_line(
@@ -763,12 +709,59 @@
     gate_table,
     out_weight,
 ):
-    query_rot, pair, key_mine, value_mine = prepare_call(
-        query_raw, key_raw, value_raw, key_cache, value_cache, norm_gain, layout, group_size
-    )
-    chosen = (jnp.arange(gate_table.shape[1]) == step_index[0]).astype(jnp.float32)
-    gates = jnp.sum(gate_table * chosen[None, :, None], 1)
-    return (attend_call(query_rot, pair, gates, out_weight), key_mine, value_mine)
+    rows, features = query_raw.shape
+    heads = group_size.shape[0]
+    hd = features // heads
+    dma = pltpu.SemaphoreType.DMA
+    in_vmem = pl.BlockSpec(memory_space=pltpu.VMEM)
+    in_smem = pl.BlockSpec(memory_space=pltpu.SMEM)
+    vmem = lambda *shape: pltpu.VMEM(shape, jnp.bfloat16)
+    wide = pltpu.VMEM((rows, hd), jnp.float32)
+    return pl.pallas_call(
+        attend_kernel,
+        out_shape=[
+            jax.ShapeDtypeStruct((rows, out_weight.shape[2]), jnp.bfloat16),
+            jax.ShapeDtypeStruct((rows, features), jnp.bfloat16),
+            jax.ShapeDtypeStruct((rows, features), jnp.bfloat16),
+        ],
+        in_specs=[in_smem] * 2 + [in_vmem] * 9 + [pl.BlockSpec(memory_space=pl.ANY)],
+        out_specs=[in_vmem] * 3,
+        scratch_shapes=[
+            vmem(heads, rows, hd),
+            pltpu.VMEM((2, out_weight.shape[2]), jnp.float32),
+        ]
+        + [wide] * 5
+        + [
+            vmem(heads, 8, 2, rows, hd),
+            vmem(heads, rows, hd),
+            vmem(heads, rows, hd),
+            vmem(heads, rows, hd),
+            vmem(2, heads, rows, hd),
+            vmem(*out_weight.shape),
+            vmem(*out_weight.shape),
+        ]
+        + [dma((heads, 4))] * 5
+        + [dma((heads,))] * 4
+        + [dma((2, heads))] * 2
+        + [dma((2, CHUNKS))] * 4
+        + [dma((2,))],
+        compiler_params=pltpu.CompilerParams(
+            collective_id=0, has_side_effects=True, vmem_limit_bytes=60 * 2**20
+        ),
+    )(
+        group_size,
+        step_index,
+        layout.astype(jnp.float32).T,
+        norm_gain.reshape(4, hd),
+        lane_tables(hd),
+        query_raw,
+        key_raw,
+        value_raw,
+        key_cache,
+        value_cache,
+        gate_table,
+        out_weight,
+    )
 
 
 def solution(mesh):

time: 104 us -> 100 us (0.962)
  Pallas kernels: 97.1 us -> 90.8 us
  local copies, waits for them, and re-layouts: 3.18 us -> 7.13 us
  other arithmetic: 2.48 us -> 0.69 us
    pallas_call x2 -> x1, Pallas kernels: 97.1 us -> 90.8 us  [on_device_line(): pl.pallas_call(attend_kernel, out_shape=[jax.ShapeDtypeStruct((rows, out_...]
    unnamed x1 -> x8, local copies, waits for them, and re-layouts: 2.36 us -> 6.3 us
    reduce_sum x1 -> x0, other arithmetic: 1.78 us -> none  [on_device_line(): gates = jnp.sum(gate_table * chosen[None, :, None], 1)]
where the time goes in v4:
time: 100 us; the launch traced here: 99.9 us
  Pallas kernels  90.8 us (91%)
  local copies, waits for them, and re-layouts  7.13 us (7%)
  between operations  1.3 us (1%)
    pallas_call x1, Pallas kernels, on_device_line(): pl.pallas_call(attend_kernel, out_shape=[jax.ShapeDtypeStruct((rows, out_...  90.8 us
    unnamed x8, local copies, waits for them, and re-layouts  6.3 us

profile of v4, /device:TPU:0, one launch (start us, length us, event | category | flops | bytes accessed | tf_op | source)
XLA Modules:
  0.0 99.9 jit_solution(9686694916565330365)
XLA Ops:
  1.3 0.7 convert_element_type.3
  2.0 0.8 copy.15
  2.8 1.8 %copy.16.gate_table = f32[2,28,1536]{2,1,0:T(8,128)} copy(f32[2,28,1536]{2,0,1:T(2,128)} %param.21) | data formatting | bytes 688128 | tf_op args[9]
  4.6 90.8 %shard_map.139 = (bf16[384,1536]{1,0:T(8,128)(2,1)}, bf16[384,768]{1,0:T(8,128)(2,1)}, bf16[384,768]{1,0:T(8,128)(2,1)}) custom-call(s32[6]{0:T(128)} %sizes.1, s32[1]{0:T(128)S(6)} %copy.20.step_index, f32[384,2]{1,0:T(8,128)} %bitcast.2, f32[4,128]{1,0:T(4,128)} %bitcast.3, f32[8,128]{1,0:T(8,128)} %constant.2.clone.table, bf16[384,768]{1,0:T(8,128)(2,1)} %query_raw.1, ...), custom_call_target="tpu_custom_call" | custom-call | tf_op jit(solution)/shard_map/pallas_call | solution.py:720
  95.4 0.0 copy-start.1
  95.4 2.4 %copy.21 = bf16[384,1536]{1,0:T(8,128)(2,1)} copy(bf16[384,1536]{1,0:T(8,128)(2,1)} %get-tuple-element.6) | data formatting | bytes 2359296
  97.8 0.0 copy-done.1
  97.8 0.0 copy-start
  97.8 0.8 copy.22
  98.6 0.5 copy-done
  99.1 0.8 copy.23
Async XLA Ops:
  95.4 2.4 %copy-start.1 = (bf16[384,768]{1,0:T(8,128)(2,1)S(1)}, bf16[384,768]{1,0:T(8,128)(2,1)}, u32[]{:S(2)}) copy-start(bf16[384,768]{1,0:T(8,128)(2,1)} %get-tuple-element.7) | copy-start | bytes 1769476
  97.8 1.3 %copy-start = (bf16[384,768]{1,0:T(8,128)(2,1)S(1)}, bf16[384,768]{1,0:T(8,128)(2,1)}, u32[]{:S(2)}) copy-start(bf16[384,768]{1,0:T(8,128)(2,1)} %get-tuple-element.8) | copy-start | bytes 1769476

commit v5 on v4

--- a/solution.py
+++ b/solution.py
@@ -229,6 +229,7 @@
     gain_q, gain_k, held, guest, mixed, returned, full, own_weight, far_weight,
     in_send, out_send, side_send, line_recv, side_recv, guest_send, guest_recv, back_send,
     back_recv, full_send, full_recv, across_send, across_recv, group_send, group_recv, load_sem,
+    lent_rows, part_out, part_in, lent_send, lent_recv, part_sem,
 ):
     heads, rows, hd = query.shape
     features, columns = weight.shape[1:]
@@ -332,6 +333,21 @@
         )
 
     straight = side == core
+    image_rows = pl.ds(text_rows, rows - text_rows)
+
+    def lend_rows(h):
+        return pltpu.make_async_remote_copy(
+            src_ref=returned.at[h, image_rows], dst_ref=lent_rows.at[h],
+            send_sem=lent_send.at[h], recv_sem=lent_recv.at[h],
+            device_id={"seq": other_core}, device_id_type=MESH,
+        )
+
+    def send_part():
+        return pltpu.make_async_remote_copy(
+            src_ref=part_out, dst_ref=part_in,
+            send_sem=part_sem.at[0], recv_sem=part_sem.at[1],
+            device_id={"tensor": 1 - side}, device_id_type=MESH,
+        )
 
     def distribute(h):
         @pl.when(straight)
@@ -343,6 +359,10 @@
         def _():
             hand_over(h, 0).start()
             hand_over(h, 1).start()
+
+        @pl.when(gives_text & (core == 0))
+        def _():
+            lend_rows(h).start()
 
     factor = hd ** (-0.5) * math.log2(math.e)
 
@@ -441,14 +461,13 @@
         lax.fori_loop(0, 4, one, 0)
 
     def start_weights():
-        @pl.when(gives_text)
-        def _():
-            across(0, 0).start()
-            across(0, 1).start()
-
-        @pl.when(jnp.logical_not(gives_text))
-        def _():
-            for c in range(CHUNKS):
+        for c in range(CHUNKS):
+            @pl.when(gives_text)
+            def _():
+                across(0, c).start()
+
+            @pl.when(jnp.logical_not(gives_text))
+            def _():
                 across(1, c).start()
 
         load(1).start()
@@ -456,6 +475,8 @@
         @pl.when(has_text)
         def _():
             load(0).start()
+
+    start_weights()
 
     @pl.when(is_end)
     def _():
@@ -474,7 +495,6 @@
             return carry
 
         lax.fori_loop(0, heads, push, 0)
-        start_weights()
 
         def step(h, carry):
             for source in (my_mid, far_mid, far_end):
@@ -492,32 +512,11 @@
             def _():
                 relay(1, h)
 
-            @pl.when(gives_text)
-            def _():
-                across(0, h).wait_send()
-
-                @pl.when(h == 0)
-                def _():
-                    across(0, 2).start()
-
-                @pl.when(h > 0)
-                def _():
-                    across(1, h - 1).start()
-
             return carry
 
         lax.fori_loop(0, shared, step, 0)
 
         def finish(h, carry):
-            @pl.when(has_text)
-            def _():
-                relay(1, h - shared)
-
-            @pl.when(gives_text & (h == shared))
-            def _():
-                across(1, 0).wait_send()
-                across(1, 2).start()
-
             give_back(h).wait_recv()
             distribute(h)
             return carry
@@ -562,7 +561,6 @@
             along(h, my_end, inner, in_send).start()
             aside(h, my_end).start()
 
-        start_weights()
         take_end(0)
 
         def step(h, carry):
@@ -620,9 +618,34 @@
 
         lax.fori_loop(0, heads, drain, 0)
 
+    width = 512
     load(1).wait()
-    for c in range(CHUNKS):
-        pass_on(1, c).wait_recv()
+
+    @pl.when(gives_text)
+    def _():
+        @pl.when(core == 0)
+        def _():
+            for h in range(heads):
+                lent_rows[h] = returned[h, text_rows:]
+
+        @pl.when(core == 1)
+        def _():
+            for h in range(heads):
+                lend_rows(h).wait_recv()
+
+        partial_rows = jnp.concatenate([lent_rows[h] for h in range(heads)], 1)
+        for first in range(0, columns, width):
+            part_out[:, first : first + width] = jnp.dot(
+                partial_rows,
+                own_weight[1, :, first : first + width],
+                preferred_element_type=jnp.float32,
+            ).astype(part_out.dtype)
+        send_part().start()
+
+    @pl.when(jnp.logical_not(has_text))
+    def _():
+        for c in range(CHUNKS):
+            pass_on(1, c).wait_recv()
 
     @pl.when(has_text)
     def _():
@@ -642,7 +665,9 @@
     lax.fori_loop(0, heads, collect, 0)
     own_rows = jnp.concatenate([full[side, h] for h in range(heads)], 1)
     far_rows = jnp.concatenate([full[1 - side, h] for h in range(heads)], 1)
-    width = 512
+    @pl.when(has_text)
+    def _():
+        send_part().wait_recv()
 
     def project(first, last, stream, place):
         sums = jnp.dot(
@@ -658,7 +683,10 @@
         @pl.when(has_text)
         def _():
             project(0, text_rows, 0, place)
-            project(text_rows, rows, 1, place)
+            sums = jnp.dot(
+                own_rows[text_rows:], own_weight[1, :, place], preferred_element_type=jnp.float32
+            ) + part_in[:, place].astype(jnp.float32)
+            out[text_rows:, place] = (sums * gates[1:2, place]).astype(out.dtype)
 
         @pl.when(jnp.logical_not(has_text))
         def _():
@@ -682,18 +710,30 @@
 
     lax.fori_loop(0, heads, drain_rows, 0)
     for c in range(CHUNKS):
-        pass_on(1, c).wait_send()
-    for c in range(1, CHUNKS):
-        across(1, c).wait_send()
-
-    @pl.when(jnp.logical_not(gives_text))
+        @pl.when(gives_text)
+        def _():
+            across(0, c).wait_send()
+
+        @pl.when(jnp.logical_not(gives_text))
+        def _():
+            across(1, c).wait_send()
+
+        @pl.when(has_text)
+        def _():
+            pass_on(0, c).wait_send()
+
+        @pl.when(jnp.logical_not(has_text))
+        def _():
+            pass_on(1, c).wait_send()
+
+    @pl.when(gives_text)
     def _():
-        across(1, 0).wait_send()
-
-    @pl.when(has_text)
-    def _():
-        for c in range(CHUNKS):
-            pass_on(0, c).wait_send()
+        send_part().wait_send()
+
+        @pl.when(core == 0)
+        def _():
+            for h in range(heads):
+                lend_rows(h).wait_send()
 
 
 def on_device_line(
@@ -712,6 +752,7 @@
     rows, features = query_raw.shape
     heads = group_size.shape[0]
     hd = features // heads
+    text_rows = rows * 8 // TEXT_PART
     dma = pltpu.SemaphoreType.DMA
     in_vmem = pl.BlockSpec(memory_space=pltpu.VMEM)
     in_smem = pl.BlockSpec(memory_space=pltpu.SMEM)
@@ -744,6 +785,13 @@
         + [dma((heads,))] * 4
         + [dma((2, heads))] * 2
         + [dma((2, CHUNKS))] * 4
+        + [dma((2,))]
+        + [
+            vmem(heads, rows - text_rows, hd),
+            vmem(rows - text_rows, out_weight.shape[2]),
+            vmem(rows - text_rows, out_weight.shape[2]),
+        ]
+        + [dma((heads,))] * 2
         + [dma((2,))],
         compiler_params=pltpu.CompilerParams(
             collective_id=0, has_side_effects=True, vmem_limit_bytes=60 * 2**20

time: 100 us -> 95.1 us (0.951)
  Pallas kernels: 90.8 us -> 85.7 us
    pallas_call x1, Pallas kernels: 90.8 us -> 85.7 us  [on_device_line(): pl.pallas_call(attend_kernel, out_shape=[jax.ShapeDtypeStruct((rows, out_...]
where the time goes in v5:
time: 95.1 us; the launch traced here: 94.8 us
  Pallas kernels  85.7 us (90%)
  local copies, waits for them, and re-layouts  7.13 us (7%)
  between operations  1.3 us (1%)
    pallas_call x1, Pallas kernels, on_device_line(): pl.pallas_call(attend_kernel, out_shape=[jax.ShapeDtypeStruct((rows, out_...  85.7 us
    unnamed x8, local copies, waits for them, and re-layouts  6.3 us

profile of v5, /device:TPU:0, one launch (start us, length us, event | category | flops | bytes accessed | tf_op | source)
XLA Modules:
  0.0 94.8 jit_solution(14859274579821375162)
XLA Ops:
  1.3 0.7 convert_element_type.3
  2.0 0.8 copy.15
  2.8 1.8 %copy.16.gate_table = f32[2,28,1536]{2,1,0:T(8,128)} copy(f32[2,28,1536]{2,0,1:T(2,128)} %param.21) | data formatting | bytes 688128 | tf_op args[9]
  4.6 85.7 %shard_map.139 = (bf16[384,1536]{1,0:T(8,128)(2,1)}, bf16[384,768]{1,0:T(8,128)(2,1)}, bf16[384,768]{1,0:T(8,128)(2,1)}) custom-call(s32[6]{0:T(128)} %sizes.1, s32[1]{0:T(128)S(6)} %copy.20.step_index, f32[384,2]{1,0:T(8,128)} %bitcast.2, f32[4,128]{1,0:T(4,128)} %bitcast.3, f32[8,128]{1,0:T(8,128)} %constant.2.clone.table, bf16[384,768]{1,0:T(8,128)(2,1)} %query_raw.1, ...), custom_call_target="tpu_custom_call" | custom-call | tf_op jit(solution)/shard_map/pallas_call | solution.py:761
  90.3 0.0 copy-start.1
  90.3 2.4 %copy.21 = bf16[384,1536]{1,0:T(8,128)(2,1)} copy(bf16[384,1536]{1,0:T(8,128)(2,1)} %get-tuple-element.6) | data formatting | bytes 2359296
  92.7 0.0 copy-done.1
  92.7 0.0 copy-start
  92.8 0.8 copy.22
  93.6 0.5 copy-done
  94.0 0.8 copy.23
Async XLA Ops:
  90.3 2.4 %copy-start.1 = (bf16[384,768]{1,0:T(8,128)(2,1)S(1)}, bf16[384,768]{1,0:T(8,128)(2,1)}, u32[]{:S(2)}) copy-start(bf16[384,768]{1,0:T(8,128)(2,1)} %get-tuple-element.7) | copy-start | bytes 1769476
  92.7 1.3 %copy-start = (bf16[384,768]{1,0:T(8,128)(2,1)S(1)}, bf16[384,768]{1,0:T(8,128)(2,1)}, u32[]{:S(2)}) copy-start(bf16[384,768]{1,0:T(8,128)(2,1)} %get-tuple-element.8) | copy-start | bytes 1769476

commit v6 on v5

--- a/solution.py
+++ b/solution.py
@@ -224,8 +224,8 @@
 
 
 def attend_kernel(
-    sizes, step_index, positions, gains, table, query_raw, key_raw, value_raw, key_old, value_old,
-    gate_table, weight, out, key_out, value_out, query, gates, cosine, sine_low, sine_high,
+    sizes, positions, gains, table, query_raw, key_raw, value_raw, key_old, value_old,
+    gates, weight, out, key_out, value_out, query, cosine, sine_low, sine_high,
     gain_q, gain_k, held, guest, mixed, returned, full, own_weight, far_weight,
     in_send, out_send, side_send, line_recv, side_recv, guest_send, guest_recv, back_send,
     back_recv, full_send, full_recv, across_send, across_recv, group_send, group_recv, load_sem,
@@ -408,8 +408,6 @@
     text = row_ids == 0
     gain_q[...] = jnp.where(text, gains[0:1, :], gains[2:3, :])
     gain_k[...] = jnp.where(text, gains[1:2, :], gains[3:4, :])
-    for stream in range(2):
-        gates[stream : stream + 1, :] = gate_table[stream, pl.ds(step_index[0], 1), :]
 
     full_mean = jnp.full((hd, hd), 1.0 / hd, jnp.float32)
     in_low = lax.broadcasted_iota(jnp.int32, (hd, hd), 0) < hd // 2
@@ -665,10 +663,6 @@
     lax.fori_loop(0, heads, collect, 0)
     own_rows = jnp.concatenate([full[side, h] for h in range(heads)], 1)
     far_rows = jnp.concatenate([full[1 - side, h] for h in range(heads)], 1)
-    @pl.when(has_text)
-    def _():
-        send_part().wait_recv()
-
     def project(first, last, stream, place):
         sums = jnp.dot(
             own_rows[first:last], own_weight[stream, :, place], preferred_element_type=jnp.float32
@@ -683,18 +677,25 @@
         @pl.when(has_text)
         def _():
             project(0, text_rows, 0, place)
+
+        @pl.when(jnp.logical_not(has_text))
+        def _():
+            project(0, rows, 1, place)
+
+        return carry
+
+    lax.fori_loop(0, columns // width, block, 0)
+
+    @pl.when(has_text)
+    def _():
+        send_part().wait_recv()
+        for first in range(0, columns, width):
+            last = first + width
             sums = jnp.dot(
-                own_rows[text_rows:], own_weight[1, :, place], preferred_element_type=jnp.float32
-            ) + part_in[:, place].astype(jnp.float32)
-            out[text_rows:, place] = (sums * gates[1:2, place]).astype(out.dtype)
-
-        @pl.when(jnp.logical_not(has_text))
-        def _():
-            project(0, rows, 1, place)
-
-        return carry
-
-    lax.fori_loop(0, columns // width, block, 0)
+                own_rows[text_rows:], own_weight[1, :, first:last],
+                preferred_element_type=jnp.float32,
+            ) + part_in[:, first:last].astype(jnp.float32)
+            out[text_rows:, first:last] = (sums * gates[1:2, first:last]).astype(out.dtype)
 
     def drain_rows(h, carry):
         @pl.when(straight)
@@ -765,11 +766,10 @@
             jax.ShapeDtypeStruct((rows, features), jnp.bfloat16),
             jax.ShapeDtypeStruct((rows, features), jnp.bfloat16),
         ],
-        in_specs=[in_smem] * 2 + [in_vmem] * 9 + [pl.BlockSpec(memory_space=pl.ANY)],
+        in_specs=[in_smem] + [in_vmem] * 9 + [pl.BlockSpec(memory_space=pl.ANY)],
         out_specs=[in_vmem] * 3,
         scratch_shapes=[
             vmem(heads, rows, hd),
-            pltpu.VMEM((2, out_weight.shape[2]), jnp.float32),
         ]
         + [wide] * 5
         + [
@@ -798,7 +798,6 @@
         ),
     )(
         group_size,
-        step_index,
         layout.astype(jnp.float32).T,
         norm_gain.reshape(4, hd),
         lane_tables(hd),
@@ -807,7 +806,7 @@
         value_raw,
         key_cache,
         value_cache,
-        gate_table,
+        lax.dynamic_index_in_dim(gate_table, step_index[0], 1, keepdims=False),
         out_weight,
     )
 

time: 95.1 us -> 92.3 us (0.971)
  Pallas kernels: 85.7 us -> 84.1 us
  local copies, waits for them, and re-layouts: 7.13 us -> 5.95 us
    unnamed x8 -> x9, local copies, waits for them, and re-layouts: 6.3 us -> 4.52 us
    pallas_call x1, Pallas kernels: 85.7 us -> 84.1 us  [on_device_line(): pl.pallas_call(attend_kernel, out_shape=[jax.ShapeDtypeStruct((rows, out_...]
where the time goes in v6:
time: 92.3 us; the launch traced here: 92 us
  Pallas kernels  84.1 us (91%)
  local copies, waits for them, and re-layouts  5.95 us (6%)
  between operations  1.36 us (1%)
    pallas_call x1, Pallas kernels, on_device_line(): pl.pallas_call(attend_kernel, out_shape=[jax.ShapeDtypeStruct((rows, out_...  84.1 us
    unnamed x9, local copies, waits for them, and re-layouts  4.52 us

profile of v6, /device:TPU:0, one launch (start us, length us, event | category | flops | bytes accessed | tf_op | source)
XLA Modules:
  0.0 92.0 jit_solution(17688112449729682067)
XLA Ops:
  0.6 0.0 copy-start
  1.3 0.7 convert_element_type.3
  2.0 0.0 copy-done
  2.0 0.6 dynamic-slice_bitcast_fusion.gates
  2.6 0.8 copy.15
  3.5 84.1 %shard_map.139 = (bf16[384,1536]{1,0:T(8,128)(2,1)}, bf16[384,768]{1,0:T(8,128)(2,1)}, bf16[384,768]{1,0:T(8,128)(2,1)}) custom-call(s32[6]{0:T(128)} %sizes.1, f32[384,2]{1,0:T(8,128)} %bitcast.8, f32[4,128]{1,0:T(4,128)} %bitcast.9, f32[8,128]{1,0:T(8,128)} %constant.8.clone.table, bf16[384,768]{1,0:T(8,128)(2,1)} %query_raw.1, bf16[384,768]{1,0:T(8,128)(2,1)} %key_raw.1, ...), custom_call_target="tpu_custom_call" | custom-call | tf_op jit(solution)/shard_map/pallas_call | solution.py:762
  87.5 0.0 copy-start.2
  87.5 2.4 %copy.20 = bf16[384,1536]{1,0:T(8,128)(2,1)} copy(bf16[384,1536]{1,0:T(8,128)(2,1)} %get-tuple-element.6) | data formatting | bytes 2359296
  90.0 0.0 copy-done.2
  90.0 0.0 copy-start.1
  90.0 0.8 copy.21
  90.8 0.5 copy-done.1
  91.2 0.8 copy.22
Async XLA Ops:
  0.6 1.4 %copy-start = (f32[2,28,1536]{2,0,1:T(2,128)S(1)}, f32[2,28,1536]{2,0,1:T(2,128)}, u32[]{:S(2)}) copy-start(f32[2,28,1536]{2,0,1:T(2,128)} %param.21) | copy-start | bytes 1032196
  87.5 2.4 %copy-start.2 = (bf16[384,768]{1,0:T(8,128)(2,1)S(1)}, bf16[384,768]{1,0:T(8,128)(2,1)}, u32[]{:S(2)}) copy-start(bf16[384,768]{1,0:T(8,128)(2,1)} %get-tuple-element.7) | copy-start | bytes 1769476
  90.0 1.3 %copy-start.1 = (bf16[384,768]{1,0:T(8,128)(2,1)S(1)}, bf16[384,768]{1,0:T(8,128)(2,1)}, u32[]{:S(2)}) copy-start(bf16[384,768]{1,0:T(8,128)(2,1)} %get-tuple-element.8) | copy-start | bytes 1769476

commit v7 on v6

--- a/solution.py
+++ b/solution.py
@@ -333,6 +333,7 @@
         )
 
     straight = side == core
+    width = 512
     image_rows = pl.ds(text_rows, rows - text_rows)
 
     def lend_rows(h):
@@ -342,10 +343,11 @@
             device_id={"seq": other_core}, device_id_type=MESH,
         )
 
-    def send_part():
+    def send_part(first):
+        place = pl.ds(first, width)
         return pltpu.make_async_remote_copy(
-            src_ref=part_out, dst_ref=part_in,
-            send_sem=part_sem.at[0], recv_sem=part_sem.at[1],
+            src_ref=part_out.at[:, place], dst_ref=part_in.at[:, place],
+            send_sem=part_sem.at[0, first // width], recv_sem=part_sem.at[1, first // width],
             device_id={"tensor": 1 - side}, device_id_type=MESH,
         )
 
@@ -616,7 +618,6 @@
 
         lax.fori_loop(0, heads, drain, 0)
 
-    width = 512
     load(1).wait()
 
     @pl.when(gives_text)
@@ -638,7 +639,7 @@
                 own_weight[1, :, first : first + width],
                 preferred_element_type=jnp.float32,
             ).astype(part_out.dtype)
-        send_part().start()
+            send_part(first).start()
 
     @pl.when(jnp.logical_not(has_text))
     def _():
@@ -688,8 +689,8 @@
 
     @pl.when(has_text)
     def _():
-        send_part().wait_recv()
         for first in range(0, columns, width):
+            send_part(first).wait_recv()
             last = first + width
             sums = jnp.dot(
                 own_rows[text_rows:], own_weight[1, :, first:last],
@@ -729,7 +730,8 @@
 
     @pl.when(gives_text)
     def _():
-        send_part().wait_send()
+        for first in range(0, columns, width):
+            send_part(first).wait_send()
 
         @pl.when(core == 0)
         def _():
@@ -792,7 +794,7 @@
             vmem(rows - text_rows, out_weight.shape[2]),
         ]
         + [dma((heads,))] * 2
-        + [dma((2,))],
+        + [dma((2, out_weight.shape[2] // 512))],
         compiler_params=pltpu.CompilerParams(
             collective_id=0, has_side_effects=True, vmem_limit_bytes=60 * 2**20
         ),

time: 92.3 us -> 92.1 us (level)
  no operation moved by 1% of the time
where the time goes in v7:
time: 92.1 us; the launch traced here: 91.9 us
  Pallas kernels  83.9 us (91%)
  local copies, waits for them, and re-layouts  5.95 us (6%)
  between operations  1.36 us (1%)
    pallas_call x1, Pallas kernels, on_device_line(): pl.pallas_call(attend_kernel, out_shape=[jax.ShapeDtypeStruct((rows, out_...  83.9 us
    unnamed x9, local copies, waits for them, and re-layouts  4.52 us

profile of v7, /device:TPU:0, one launch (start us, length us, event | category | flops | bytes accessed | tf_op | source)
XLA Modules:
  0.0 91.9 jit_solution(16519814730022195360)
XLA Ops:
  0.6 0.0 copy-start
  1.3 0.7 convert_element_type.3
  2.0 0.0 copy-done
  2.0 0.6 dynamic-slice_bitcast_fusion.gates
  2.6 0.8 copy.15
  3.5 83.9 %shard_map.139 = (bf16[384,1536]{1,0:T(8,128)(2,1)}, bf16[384,768]{1,0:T(8,128)(2,1)}, bf16[384,768]{1,0:T(8,128)(2,1)}) custom-call(s32[6]{0:T(128)} %sizes.1, f32[384,2]{1,0:T(8,128)} %bitcast.8, f32[4,128]{1,0:T(4,128)} %bitcast.9, f32[8,128]{1,0:T(8,128)} %constant.8.clone.table, bf16[384,768]{1,0:T(8,128)(2,1)} %query_raw.1, bf16[384,768]{1,0:T(8,128)(2,1)} %key_raw.1, ...), custom_call_target="tpu_custom_call" | custom-call | tf_op jit(solution)/shard_map/pallas_call | solution.py:764
  87.4 0.0 copy-start.2
  87.4 2.4 %copy.20 = bf16[384,1536]{1,0:T(8,128)(2,1)} copy(bf16[384,1536]{1,0:T(8,128)(2,1)} %get-tuple-element.6) | data formatting | bytes 2359296
  89.8 0.0 copy-done.2
  89.8 0.0 copy-start.1
  89.8 0.8 copy.21
  90.6 0.5 copy-done.1
  91.1 0.8 copy.22
Async XLA Ops:
  0.6 1.4 %copy-start = (f32[2,28,1536]{2,0,1:T(2,128)S(1)}, f32[2,28,1536]{2,0,1:T(2,128)}, u32[]{:S(2)}) copy-start(f32[2,28,1536]{2,0,1:T(2,128)} %param.21) | copy-start | bytes 1032196
  87.4 2.4 %copy-start.2 = (bf16[384,768]{1,0:T(8,128)(2,1)S(1)}, bf16[384,768]{1,0:T(8,128)(2,1)}, u32[]{:S(2)}) copy-start(bf16[384,768]{1,0:T(8,128)(2,1)} %get-tuple-element.7) | copy-start | bytes 1769476
  89.8 1.3 %copy-start.1 = (bf16[384,768]{1,0:T(8,128)(2,1)S(1)}, bf16[384,768]{1,0:T(8,128)(2,1)}, u32[]{:S(2)}) copy-start(bf16[384,768]{1,0:T(8,128)(2,1)} %get-tuple-element.8) | copy-start | bytes 1769476
